TPU v7x, 256 devices: a whole 4x4x8 slice. The times are simulated.
256 devices in a mesh: gx: 16 (over z, core), gy: 16 (over x, y).
Axes of the slice: x: 4, y: 4, z: 8, core: 2. Of those that a mesh axis runs over, the one named last changes fastest.
Arguments:
- positions: float32 [16, 16, 3, 256], P('gx', 'gy'), may hold values from 0 to 10
- species: int32 [16, 16, 256], P('gx', 'gy'), may hold values from 0 to 5
- neighbours: int32 [16, 16, 256, 12], P('gx', 'gy'), may hold values from 0 to 2303
- counts: int32 [16, 16, 256], P('gx', 'gy'), may hold values from 6 to 12
- species_embed: float32 [6, 128], replicated, may hold values from -6 to 6
- radial: float32 [2, 2, 8, 128], replicated, may hold values from -2 to 2
- mixing: float32 [2, 2, 128, 128], replicated, may hold values from -0.5 to 0.5
- read_hidden: float32 [128, 128], replicated, may hold values from -0.5 to 0.5
- read_out: float32 [128], replicated, may hold values from -0.5 to 0.5
- charge_map: float32 [128, 64], replicated, may hold values from -0.5 to 0.5
- wavevectors: int32 [3, 4096], replicated, may hold values from -8 to 8, as said below
Outputs:
- forces: float32 [16, 16, 3, 256], P('gx', 'gy')
- site_energy: float32 [16, 16, 256], P('gx', 'gy')
Inputs may be any that keep to these rules, and one draw needn't show every extreme that they name: `neighbours`: entry (3 a + b) * 256 + t names atom t of the cell offset by (a - 1, b - 1) along gx, gy, periodically. Slots n < counts are used. `wavevectors`: the 4096 triples are distinct, and no triple has its first two components both zero.
All inputs are finite; a program needn't handle non-finite values.
Results may differ from a plain program's by a relative error of at most 0.0017.
Values may be sent and summed in bfloat16 or wider, within the bound.
A program may use at most 128 MiB of HBM per device.

v0:
```python
import math

import jax
import jax.numpy as jnp
from jax import lax
from jax.sharding import PartitionSpec as P

cell_width = 10.0
box_height = 30.0
cut_radius = 50.0
soften = 0.25
screen = 0.5
smear_width = 0.5
highest = lax.Precision.HIGHEST


def passed_along(block, axis, distance):
    devices = range(lax.axis_size(axis))
    route = [((i - distance) % len(devices), i) for i in devices]
    return lax.ppermute(block, axis, route)


def with_halo(block, sides, width):
    for axis, dim in sides:
        count = lax.axis_size(axis)
        forward = [(i, i + 1) for i in range(count - 1)]
        forward.append((count - 1, 0))
        backward = [(target, source) for source, target in forward]
        low = lax.ppermute(
            lax.slice_in_dim(block, block.shape[dim] - width, None, axis=dim), axis, forward
        )
        high = lax.ppermute(lax.slice_in_dim(block, 0, width, axis=dim), axis, backward)
        block = jnp.concatenate([low, block, high], axis=dim)
    return block


def build_frame(extended):
    offsets = (jnp.arange(3, dtype=jnp.float32) - 1.0) * cell_width
    shift_x = jnp.broadcast_to(offsets[:, None], (3, 3))
    shift_y = jnp.broadcast_to(offsets[None, :], (3, 3))
    shifts = jnp.stack([shift_x, shift_y, jnp.zeros((3, 3), jnp.float32)], axis=2)
    coords = extended[:, :, :3, :] + shifts[:, :, :, None]
    src_pos = jnp.moveaxis(coords, 2, 0).reshape(3, -1)
    kind_codes = extended[:, :, 3, :].reshape(-1)
    return (src_pos, kind_codes)


def embed_rows(kind_codes, species_embed):
    lookup = (
        kind_codes[:, None] == jnp.arange(species_embed.shape[0], dtype=jnp.float32)[None, :]
    ).astype(jnp.float32)
    return jnp.dot(lookup, species_embed, precision=highest)


def interact(h_dst, h_src, own_pos, src_pos, neighbour_ids, slot_counts, radial_pair, mix_pair):
    slots = neighbour_ids.shape[1]
    orders = radial_pair.shape[1]
    relative = src_pos[:, neighbour_ids] - own_pos[:, :, None]
    distance = jnp.sqrt(jnp.sum(relative * relative, axis=0) + soften)
    unit_vec = relative / distance[None]
    frequency = jnp.arange(1, orders + 1, dtype=jnp.float32) * (math.pi / cut_radius)
    arg_scaled = distance[:, :, None] * frequency
    radial_basis = jnp.sin(arg_scaled) / arg_scaled
    live_slots = (jnp.arange(slots)[None, :] < slot_counts[:, None]).astype(jnp.float32)
    weight_zero = (
        jnp.einsum("anr,rc->anc", radial_basis, radial_pair[0], precision=highest)
        * live_slots[:, :, None]
    )
    weight_one = (
        jnp.einsum("anr,rc->anc", radial_basis, radial_pair[1], precision=highest)
        * live_slots[:, :, None]
    )
    source = h_src[neighbour_ids]
    norm_factor = 1.0 / math.sqrt(slots)
    msg_zero = jnp.sum(weight_zero * source, axis=1) * norm_factor
    msg_one = (
        jnp.einsum("anc,xan->xac", weight_one * source, unit_vec, precision=highest) * norm_factor
    )
    squares = jnp.sum(msg_one * msg_one, axis=0)
    preact = jnp.dot(msg_zero, mix_pair[0], precision=highest) + jnp.dot(
        squares, mix_pair[1], precision=highest
    )
    return h_dst + jax.nn.silu(preact)


def first_layer(own_pos, src_pos, initial_src, neighbour_ids, slot_counts, radial, mixing):
    atom_count = own_pos.shape[1]
    return interact(
        initial_src[4 * atom_count : 5 * atom_count],
        initial_src,
        own_pos,
        src_pos,
        neighbour_ids,
        slot_counts,
        radial[0],
        mixing[0],
    )


def second_section(
    hidden_src,
    own_pos,
    src_pos,
    neighbour_ids,
    slot_counts,
    radial,
    mixing,
    read_hidden,
    read_out,
    charge_map,
):
    atom_count = own_pos.shape[1]
    hidden_two = interact(
        hidden_src[4 * atom_count : 5 * atom_count],
        hidden_src,
        own_pos,
        src_pos,
        neighbour_ids,
        slot_counts,
        radial[1],
        mixing[1],
    )
    energy = jnp.dot(
        jax.nn.silu(jnp.dot(hidden_two, read_hidden, precision=highest)),
        read_out,
        precision=highest,
    )
    charges = jnp.dot(hidden_two, charge_map, precision=highest)
    return (energy, charges)


def wave_terms(wavevectors, grid_x, grid_y):
    lengths = jnp.array([grid_x * cell_width, grid_y * cell_width, box_height], dtype=jnp.float32)
    wave_phys = 2.0 * math.pi * wavevectors.astype(jnp.float32) / lengths[:, None]
    wave_sq = jnp.sum(wave_phys * wave_phys, axis=0)
    green_weight = jnp.exp(-smear_width * wave_sq) / (wave_sq + screen * screen)
    return (wave_phys, green_weight)


def phase_pair(global_pos, wave_part):
    angle = (
        global_pos[0][:, None] * wave_part[0][None, :]
        + global_pos[1][:, None] * wave_part[1][None, :]
        + global_pos[2][:, None] * wave_part[2][None, :]
    )
    return (jnp.cos(angle), jnp.sin(angle))


def structure_term(charges, global_pos, wave_part):
    cosine, sine_part = phase_pair(global_pos, wave_part)
    dims = (((0,), (0,)), ((), ()))
    real_part = lax.dot_general(cosine, charges, dims, precision=highest)
    imag_part = lax.dot_general(sine_part, charges, dims, precision=highest)
    return jnp.concatenate([real_part, imag_part], axis=1)


def fold_terms(carried, piece_rows, start_row, charges, global_pos, wave_phys):
    potential, lr_grad = carried
    row_count = piece_rows.shape[0]
    lat_width = charges.shape[1]
    wave_part = lax.dynamic_slice_in_dim(
        wave_phys, jnp.asarray(start_row).astype(jnp.int32), row_count, 1
    )
    cosine, sine_part = phase_pair(global_pos, wave_part)
    weight_re = piece_rows[:, :lat_width]
    weight_im = piece_rows[:, lat_width:]
    potential = (
        potential
        + jnp.dot(cosine, weight_re, precision=highest)
        + jnp.dot(sine_part, weight_im, precision=highest)
    )
    dims = (((1,), (1,)), ((), ()))
    proj_re = lax.dot_general(charges, weight_re, dims, precision=highest)
    proj_im = lax.dot_general(charges, weight_im, dims, precision=highest)
    phase_turn = cosine * proj_im - sine_part * proj_re
    lr_grad = lr_grad + lax.dot_general(wave_part, phase_turn, dims, precision=highest)
    return (potential, lr_grad)


def send_back(cotangent_grid):
    column = cotangent_grid[:, 1]
    for shift_by, column_pick in ((1, 2), (-1, 0)):
        column = column + passed_along(cotangent_grid[:, column_pick], "gy", shift_by)
    running = column[1]
    for shift_by, column_pick in ((1, 2), (-1, 0)):
        running = running + passed_along(column[column_pick], "gx", shift_by)
    return running


def per_device(
    positions,
    species,
    neighbours,
    counts,
    species_embed,
    radial,
    mixing,
    read_hidden,
    read_out,
    charge_map,
    wavevectors,
):
    atom_count = positions.shape[3]
    width = read_hidden.shape[0]
    lat_width = charge_map.shape[1]
    wave_count = wavevectors.shape[1]
    own_pos = positions[0, 0]
    neighbour_ids = neighbours[0, 0]
    slot_counts = counts[0, 0]
    packed = jnp.concatenate([positions, species.astype(jnp.float32)[:, :, None, :]], axis=2)
    extended = with_halo(packed, (("gx", 0), ("gy", 1)), 1)
    src_pos, kind_codes = build_frame(extended)
    initial_src = embed_rows(kind_codes, species_embed)

    def layer_one(own_coords, source_coords):
        return first_layer(
            own_coords, source_coords, initial_src, neighbour_ids, slot_counts, radial, mixing
        )

    hidden_one, pull_one = jax.vjp(layer_one, own_pos, src_pos)
    hidden_low = hidden_one.astype(jnp.bfloat16)
    ghost_hidden = with_halo(hidden_low[None, None], (("gx", 0), ("gy", 1)), 1)
    hidden_src = ghost_hidden.reshape(9 * atom_count, width).astype(jnp.float32)

    def section_two(source_hidden, own_coords, source_coords):
        return second_section(
            source_hidden,
            own_coords,
            source_coords,
            neighbour_ids,
            slot_counts,
            radial,
            mixing,
            read_hidden,
            read_out,
            charge_map,
        )

    (energy_sr, charges), pull_two = jax.vjp(section_two, hidden_src, own_pos, src_pos)
    grid_x = lax.axis_size("gx")
    grid_y = lax.axis_size("gy")
    row_index = lax.axis_index("gx")
    col_index = lax.axis_index("gy")
    anchor = jnp.stack(
        [
            row_index.astype(jnp.float32) * cell_width,
            col_index.astype(jnp.float32) * cell_width,
            jnp.zeros((), jnp.float32),
        ]
    )
    global_pos = own_pos + anchor[:, None]
    wave_phys, green_weight = wave_terms(wavevectors, grid_x, grid_y)
    start_state = (
        jnp.zeros((atom_count, lat_width), jnp.float32),
        jnp.zeros((3, atom_count), jnp.float32),
    )

    def fold_piece(carried, piece_rows, start_row):
        return fold_terms(carried, piece_rows, start_row, charges, global_pos, wave_phys)

    block_rows = math.gcd(wave_count, 512)
    block_total = wave_count // block_rows

    def term_block(block_idx):
        return structure_term(
            charges,
            global_pos,
            lax.dynamic_slice_in_dim(wave_phys, block_idx * block_rows, block_rows, 1),
        )

    partial_sf = lax.map(term_block, jnp.arange(block_total)).reshape(wave_count, 2 * lat_width)
    structure = lax.psum(partial_sf, ("gx", "gy"))
    weighted = green_weight[:, None] * structure

    def fold_block(block_idx, carried):
        start_row = block_idx * block_rows
        return fold_piece(
            carried, lax.dynamic_slice_in_dim(weighted, start_row, block_rows, 0), start_row
        )

    potential, lr_grad = lax.fori_loop(0, block_total, fold_block, start_state)
    lr_scale = 1.0 / math.sqrt(wave_count * lat_width * atom_count * grid_x * grid_y)
    site_energy = energy_sr + lr_scale * jnp.sum(charges * potential, axis=1)
    grad_hidden, grad_own_two, grad_src_two = pull_two(
        (jnp.ones_like(energy_sr), 2.0 * lr_scale * potential)
    )
    grad_hidden_own = send_back(grad_hidden.reshape(3, 3, atom_count, width))
    grad_own_one, grad_src_one = pull_one(grad_hidden_own)
    grad_src = jnp.moveaxis((grad_src_one + grad_src_two).reshape(3, 3, 3, atom_count), 0, 2)
    grad_back = send_back(grad_src)
    forces = -(grad_own_one + grad_own_two + grad_back + 2.0 * lr_scale * lr_grad)
    return (forces[None, None], site_energy[None, None])


def solution(mesh):
    in_specs = (
        P("gx", "gy", None, None),
        P("gx", "gy", None),
        P("gx", "gy", None, None),
        P("gx", "gy", None),
        P(),
        P(),
        P(),
        P(),
        P(),
        P(),
        P(),
    )
    out_specs = (P("gx", "gy", None, None), P("gx", "gy", None))
    return jax.shard_map(
        per_device, mesh=mesh, in_specs=in_specs, out_specs=out_specs, check_vma=False
    )
```

profile of v0, /device:TPU:1, one launch (start us, length us, event | category | flops | bytes accessed | tf_op | source)
XLA Modules:
  0.0 657.0 jit_solution(15282596504475978514)
XLA Ops:
  8.6 3.2 collective-permute-start.1
  16.8 5.0 collective-permute-start.3
  23.3 4.4 collective-permute-done.2
  28.9 8.1 %gather_fusion = f32[3072,3]{1,0:T(8,128)S(1)} fusion(f32[3,2304]{0,1:T(8,128)S(1)} %bitcast.271, s32[3072]{0:T(1024)S(1)} %broadcast_clamp_fusion), kind=kCustom, calls=%fused_computation | custom fusion | bytes 86016 | tf_op jit(solution)/shard_map/jvp()/gather | solution.py:58
  41.1 10.8 %gather_fusion.1 = f32[3072,128]{1,0:T(8,128)} fusion(f32[2304,128]{1,0:T(8,128)S(1)} %fusion.133, s32[3072]{0:T(1024)S(1)} %broadcast_clamp_fusion), kind=kCustom, calls=%fused_computation.1 | custom fusion | bytes 3158016 | tf_op jit(solution)/shard_map/jvp()/gather | solution.py:73
  53.5 4.2 multiply_reduce_fusion.1
  57.8 4.4 multiply_multiply_fusion
  62.5 4.0 multiply_reduce_fusion.3
  66.8 5.0 collective-permute-start.5
  75.8 5.0 convolution_multiply_fusion.1
  82.9 10.8 %gather_fusion.2 = f32[3072,128]{1,0:T(8,128)} fusion(f32[2304,128]{1,0:T(8,128)S(1)} %bitcast_convert_fusion, s32[3072]{0:T(1024)S(1)} %broadcast_clamp_fusion), kind=kCustom, calls=%fused_computation.2 | custom fusion | bytes 3158016 | tf_op jit(solution)/shard_map/jvp()/gather | solution.py:73
  95.2 6.9 %copy_multiply_fusion.1 = (f32[256,12,128]{2,0,1:T(8,128)S(1)}, f32[256,128]{1,0:T(8,128)S(1)}, f32[256,12,128]{2,0,1:T(8,128)}) fusion(f32[256,12,128]{2,1,0:T(8,128)S(1)} %reshape.168, f32[256,12,128]{2,0,1:T(8,128)} %convolution_multiply_fusion.1, f32[256,12]{0,1:T(8,128)S(1)} %fusion.161, f32[2,2,8,128]{3,2,1,0:T(8,128)} %param.21, ...), kind=kOutput, calls=%fused_computation.121 | convolution fusion | flops 39337984 | bytes 6451232 | tf_op jit(solution)/shard_map/jvp(anr,rc->anc)/dot_general | solution.py:70
  102.4 3.9 multiply_reduce_fusion.2
  107.6 62.1 %while.26 = (s32[]{:T(128)}, f32[8,512,128]{2,1,0:T(8,128)}, f32[3,256]{1,0:T(4,128)S(1)}, s32[8]{0:T(128)S(1)}, f32[3,4096]{1,0:T(4,128)}, /*index=5*/f32[256,6...) while((s32[]{:T(128)}, f32[8,512,128]{2,1,0:T(8,128)}, ...), condition=%wide.region_7.8_spmd, body=%wide.region_6.7_spmd.sunk | while | flops 202702848 | bytes 2003167 | solution.py:271
  171.4 256.4 %all-reduce.3.cloned.1.call-done = f32[4096,128]{1,0:T(8,128)} async-done(((f32[4096,128]{1,0:T(8,128)}), f32[4096,128]{1,0:T(8,128)}) %all-reduce.3.cloned.1.call-update) | async-done | bytes 2097168 | tf_op jit(solution)/shard_map/psum | solution.py:272
  430.0 87.4 %while.27 = (s32[]{:T(128)}, f32[256,64]{0,1:T(8,128)S(1)}, f32[3,256]{1,0:T(4,128)S(1)}, f32[3,256]{1,0:T(4,128)S(1)}, f32[3,4096]{1,0:T(4,128)}, /*index=5*/f3...) while((s32[]{:T(128)}, f32[256,64]{0,1:T(8,128)S(1)}, ...), condition=%wide.region_10.11_spmd.clone, body=%wide.region_9.10_spmd.clone.sunk | while | flops 410437120 | bytes 3739922 | solution.py:281
  519.5 4.0 fusion.88
  528.7 17.4 %scatter_fusion = f32[2304,128]{1,0:T(8,128)S(1)} fusion(f32[2304,128]{1,0:T(8,128)S(1)} %pad.3, s32[3072]{0:T(1024)S(1)} %reshape.153, f32[3072,128]{1,0:T(8,128)S(1)} %reshape.179), kind=kCustom, calls=%fused_computation.3 | custom fusion | flops 393216 | bytes 4730880 | tf_op jit(solution)/shard_map/transpose(jvp())/scatter-add | solution.py:73
  547.4 3.6 collective-permute-start.9
  555.0 3.0 collective-permute-done.8
  558.1 4.4 collective-permute-start.10
  562.5 3.7 fusion.125
  568.2 4.1 fusion.47
  572.3 5.3 fusion.89
  577.6 6.2 fusion.80
  587.0 3.9 fusion.52
  591.0 3.1 fusion.122
  594.4 3.0 fusion.201
  598.6 17.2 %scatter_custom_fusion.1 = f32[3,2304]{0,1:T(8,128)S(1)} fusion(s32[3072]{0:T(1024)S(1)} %reshape.153, f32[3072,3]{1,0:T(8,128)S(1)} %copy.264, f32[]{:T(128)} %constant.47.clone.1), kind=kCustom, calls=%fused_computation.107 | custom fusion | flops 9216 | bytes 27652 | tf_op jit(solution)/shard_map/transpose(jvp())/scatter-add | solution.py:58
  617.5 17.5 %scatter_custom_fusion.2 = f32[3,2304]{0,1:T(8,128)S(1)} fusion(s32[3072]{0:T(1024)S(1)} %reshape.153, f32[3072,3]{1,0:T(8,128)} %copy.266, f32[]{:T(128)} %constant.47.clone.1), kind=kCustom, calls=%fused_computation.105 | custom fusion | flops 9216 | bytes 28160 | tf_op jit(solution)/shard_map/transpose(jvp())/scatter-add | solution.py:58
  638.0 4.9 collective-permute-start.13
  646.8 2.6 collective-permute-done.15
  (340 shorter events, 199.4 us)
Async XLA Ops:
  7.2 164.0 %copy-start = (f32[128,128]{1,0:T(8,128)S(1)}, f32[128,128]{1,0:T(8,128)}, u32[]{:S(2)}) copy-start(f32[128,128]{1,0:T(8,128)} %param.23) | copy-start | bytes 196612
  7.2 420.6 %all-reduce.3.cloned.1.call-start = ((), (), s32[]{:S(2)}) async-start(), calls=%async_computation | async-start | bytes 4194304 | tf_op jit(solution)/shard_map/psum | solution.py:272
  8.6 7.3 %collective-permute-start.1 = (f32[1,1,4,256]{3,1,2,0:T(1,128)S(1)}, f32[1,1,4,256]{3,1,2,0:T(1,128)S(1)}, u32[]{:S(2)}, u32[]{:S(2)}) collective-permute-start(f32[1,1,4,256]{3,1,2,0:T(1,128)S(1)} %pad_maximum_fusion.5), channel_id=1, source_target_pairs={{16,0},{32,16},{48,32},{64,48},{80,64},{96,80},{112,96},{128,112},... | collective-permute-start | bytes 12296 | tf_op jit(solution)/shard_map/ppermute | solution.py:32
  11.8 4.2 collective-permute-start
  16.8 6.5 collective-permute-start.3
  21.8 5.9 collective-permute-start.2
  53.5 8.6 %copy-start.4 = (f32[256,12,128]{2,1,0:T(8,128)}, f32[256,12,128]{2,1,0:T(8,128)S(1)}, u32[]{:S(2)}) copy-start(f32[256,12,128]{2,1,0:T(8,128)S(1)} %reshape.160) | copy-start | bytes 4718596
  62.5 9.3 %copy-start.39 = (f32[1,1,3,256]{3,1,2,0:T(1,128)S(1)}, f32[1,1,3,256]{3,1,2,0:T(1,128)}, u32[]{:S(2)}) copy-start(f32[1,1,3,256]{3,1,2,0:T(1,128)} %param.16) | copy-start | bytes 9220
  62.5 9.3 %copy-start.48 = (f32[3]{0:T(128)S(1)}, f32[3]{0:T(128)}, u32[]{:S(2)}) copy-start(f32[3]{0:T(128)} %pad_maximum_fusion.6) | copy-start | bytes 40
  66.7 16.0 %copy-start.17 = (f32[256,128]{1,0:T(8,128)}, f32[256,128]{1,0:T(8,128)S(1)}, u32[]{:S(2)}) copy-start(f32[256,128]{1,0:T(8,128)S(1)} %convolution_add_fusion.5) | copy-start | bytes 393220
  66.8 5.9 collective-permute-start.5
  71.8 2.1 collective-permute-start.4
  73.9 6.9 %collective-permute-start.7 = (bf16[3,1,256,128]{3,2,1,0:T(8,128)(2,1)S(1)}, bf16[3,1,256,128]{3,2,1,0:T(8,128)(2,1)S(1)}, u32[]{:S(2)}, u32[]{:S(2)}) collective-permute-start(bf16[3,1,256,128]{3,2,1,0:T(8,128)(2,1)S(1)} %pad_maximum_fusion.1), channel_id=1, source_target_pairs={{1,0},{2,1},{3,2},{4,3},{5,4},{6,5},{7,6},{8,7},{9,8},{10,9},{11,1... | collective-permute-start | bytes 589832 | tf_op jit(solution)/shard_map/ppermute | solution.py:32
  74.4 8.2 %collective-permute-start.6 = (bf16[3,1,256,128]{3,2,1,0:T(8,128)(2,1)S(1)}, bf16[3,1,256,128]{3,2,1,0:T(8,128)(2,1)S(1)}, u32[]{:S(2)}, u32[]{:S(2)}) collective-permute-start(bf16[3,1,256,128]{3,2,1,0:T(8,128)(2,1)S(1)} %pad_maximum_fusion.1), channel_id=1, source_target_pairs={{0,1},{1,2},{2,3},{3,4},{4,5},{5,6},{6,7},{7,8},{8,9},{9,10},{10,1... | collective-permute-start | bytes 589832 | tf_op jit(solution)/shard_map/ppermute | solution.py:29
  171.4 346.4 %copy-start.52 = (f32[256,128]{1,0:T(8,128)}, f32[256,128]{1,0:T(8,128)S(1)}, u32[]{:S(2)}) copy-start(f32[256,128]{1,0:T(8,128)S(1)} %fusion.196) | copy-start | bytes 393220
  430.0 88.0 %copy-start.50 = (f32[128]{0:T(128)S(1)}, f32[128]{0:T(128)}, u32[]{:S(2)}) copy-start(f32[128]{0:T(128)} %param.24) | copy-start | bytes 1540
  430.0 88.3 %copy-start.21 = (f32[2,2,128,128]{3,2,1,0:T(8,128)S(1)}, f32[2,2,128,128]{3,2,1,0:T(8,128)}, u32[]{:S(2)}) copy-start(f32[2,2,128,128]{3,2,1,0:T(8,128)} %param.22) | copy-start | bytes 786436
  528.7 22.3 %copy-start.51 = (f32[128]{0:T(128)S(1)}, f32[128]{0:T(128)}, u32[]{:S(2)}) copy-start(f32[128]{0:T(128)} %param.24) | copy-start | bytes 1540
  546.1 11.8 %collective-permute-start.8 = (f32[3,256,128]{2,1,0:T(8,128)S(1)}, f32[3,256,128]{2,1,0:T(8,128)S(1)}, u32[]{:S(2)}, u32[]{:S(2)}) collective-permute-start(f32[3,256,128]{2,1,0:T(8,128)S(1)} %get-tuple-element.335), channel_id=1, source_target_pairs={{15,0},{0,1},{1,2},{2,3},{3,4},{4,5},{5,6},{6,7},{7,8},{8,9},{9,10... | collective-permute-start | bytes 1179656 | tf_op jit(solution)/shard_map/ppermute | solution.py:20
  547.4 10.6 %collective-permute-start.9 = (f32[3,256,128]{2,1,0:T(8,128)S(1)}, f32[3,256,128]{2,1,0:T(8,128)S(1)}, u32[]{:S(2)}, u32[]{:S(2)}) collective-permute-start(f32[3,256,128]{2,1,0:T(8,128)S(1)} %get-tuple-element.336), channel_id=1, source_target_pairs={{1,0},{2,1},{3,2},{4,3},{5,4},{6,5},{7,6},{8,7},{9,8},{10,9},{11,1... | collective-permute-start | bytes 1179656 | tf_op jit(solution)/shard_map/ppermute | solution.py:20
  552.7 9.8 %copy-start.15 = (f32[256,12,128]{2,1,0:T(8,128)S(1)}, f32[256,12,128]{2,1,0:T(8,128)}, u32[]{:S(2)}) copy-start(f32[256,12,128]{2,1,0:T(8,128)} %copy-done.14) | copy-start | bytes 4718596
  558.1 8.1 %collective-permute-start.10 = (f32[256,128]{1,0:T(8,128)S(1)}, f32[256,128]{1,0:T(8,128)S(1)}, u32[]{:S(2)}, u32[]{:S(2)}) collective-permute-start(f32[256,128]{1,0:T(8,128)S(1)} %get-tuple-element.339), channel_id=1, source_target_pairs={{240,0},{0,16},{16,32},{32,48},{48,64},{64,80},{80,96},{96,112},{1... | collective-permute-start | bytes 393224 | tf_op jit(solution)/shard_map/ppermute | solution.py:20
  562.5 4.4 collective-permute-start.11
  577.6 9.4 %copy-start.5 = (f32[256,12,128]{2,1,0:T(8,128)S(1)}, f32[256,12,128]{2,1,0:T(8,128)}, u32[]{:S(2)}) copy-start(f32[256,12,128]{2,1,0:T(8,128)} %copy-done.4) | copy-start | bytes 4718596
  635.0 7.8 %copy-start.33 = (f32[256,64]{0,1:T(8,128)S(1)}, f32[256,64]{0,1:T(8,128)}, u32[]{:S(2)}) copy-start(f32[256,64]{0,1:T(8,128)} %copy-done.32) | copy-start | bytes 196612
  635.0 7.8 %copy-start.35 = (f32[256,64]{0,1:T(8,128)S(1)}, f32[256,64]{0,1:T(8,128)}, u32[]{:S(2)}) copy-start(f32[256,64]{0,1:T(8,128)} %copy-done.34) | copy-start | bytes 196612
  635.1 11.0 %copy-start.49 = (f32[1,256]{1,0:T(1,128)S(1)}, f32[1,256]{1,0:T(1,128)}, u32[]{:S(2)}) copy-start(f32[1,256]{1,0:T(1,128)} %fusion.112) | copy-start | bytes 3076
  635.1 11.5 %copy-start.31 = (f32[3,256]{0,1:T(8,128)S(1)}, f32[3,256]{0,1:T(8,128)}, u32[]{:S(2)}) copy-start(f32[3,256]{0,1:T(8,128)} %get-tuple-element.317) | copy-start | bytes 9220
  637.9 6.0 collective-permute-start.12
  638.0 5.9 collective-permute-start.13
  643.9 2.9 collective-permute-start.14
  646.0 3.3 collective-permute-start.15
  (38 other events, 151.5 us)
Sparse Core Ops, SparseCore 0:
  169.8 257.9 all-reduce.2
where the time goes:
time: 664 us; the launch traced here: 657 us
  waiting for transfers between devices  272 us (41%)
  matrix products  184 us (28%)
  local copies, waits for them, and re-layouts  78.5 us (12%)
  other arithmetic  68.7 us (10%)
  starting transfers between devices  31.6 us (5%)
  between operations  15.2 us (2%)
    psum x1, waiting for transfers between devices, per_device(): structure = lax.psum(partial_sf, ('gx', 'gy'))  256 us
    scatter-add x2, other arithmetic, interact(): relative = src_pos[:, neighbour_ids] - own_pos[:, :, None]  34.7 us
    dot_general x6, matrix products, interact(): jnp.einsum('anc,xan->xac', weight_one * source, unit_vec, precision=highest)  27.5 us
    gather x4, local copies, waits for them, and re-layouts, interact(): source = h_src[neighbour_ids]  24.7 us
    dot_general x4, matrix products, interact(): jnp.einsum('anr,rc->anc', radial_basis, radial_pair[1], precision=highest)  18.9 us
    dot_general x8, matrix products, structure_term(): imag_part = lax.dot_general(sine_part, charges, dims, precision=highest)  18.9 us
    dot_general x8, matrix products, fold_terms(): jnp.dot(sine_part, weight_im, precision=highest)  18.7 us
    dot_general x8, matrix products, structure_term(): real_part = lax.dot_general(cosine, charges, dims, precision=highest)  18.7 us
  transfers between devices with their start and end apart: 17, of which 10 were waited for; matrix products, arithmetic and copies ran while one was open for 3% of the time, Pallas kernels for 0%

commit v1 on v0

v1 whole, which is shorter than its diff:
```python
import functools
import math

import jax
import jax.numpy as jnp
from jax import lax
from jax.experimental import pallas as pl
from jax.experimental.pallas import tpu as pltpu
from jax.sharding import PartitionSpec as P

MESH = pl.DeviceIdType.MESH
f32, bf16 = jnp.float32, jnp.bfloat16
NN, NT, TN = ((1,), (0,)), ((1,), (1,)), ((0,), (0,))
CELL, HEIGHT, CUT = 10.0, 30.0, 50.0
AT, NB, C, NR, NS = 256, 12, 128, 8, 6
E = AT * NB
HALF = 1280
KZ = 9
LANES = 384
NORM = 1.0 / math.sqrt(NB)


def dot(a, b, dims):
    return lax.dot_general(a, b, (dims, ((), ())), preferred_element_type=f32)


def split2(x):
    hi = x.astype(bf16)
    return hi, (x - hi.astype(f32)).astype(bf16)


def split3(x):
    hi = x.astype(bf16)
    rest = x - hi.astype(f32)
    mid = rest.astype(bf16)
    return hi, mid, (rest - mid.astype(f32)).astype(bf16)


def dot3(a, b, dims):
    ah, al = split2(a)
    bh, bl = split2(b)
    return dot(ah, bh, dims) + dot(ah, bl, dims) + dot(al, bh, dims)


def rowid(shape):
    return lax.broadcasted_iota(jnp.int32, shape, 0)


def laneid(shape):
    return lax.broadcasted_iota(jnp.int32, shape, 1)


def sigmoid(x):
    return 1.0 / (1.0 + jnp.exp(-x))


def silu_pair(x):
    s = sigmoid(x)
    return x * s, s * (1.0 + x * (1.0 - s))


def swap_rows(x):
    h = x.shape[0] // 2
    return jnp.concatenate([x[h:], x[:h]], axis=0)


def swap_lanes(x):
    h = x.shape[1] // 2
    return jnp.concatenate([x[:, h:], x[:, :h]], axis=1)


def colsum(x):
    return jnp.sum(x, axis=0, keepdims=True)


def one_hot(idx_row):
    f = jnp.where(idx_row >= HALF, idx_row - HALF, idx_row)
    return jnp.where(rowid((HALF, AT)) == f, 1.0, 0.0).astype(bf16)


def pos_table(frame):
    cells = []
    for s in range(9):
        a, b = divmod(s, 3)
        r = rowid((8, AT))
        shift = jnp.where(r == 0, CELL * (a - 1), 0.0) + jnp.where(r == 1, CELL * (b - 1), 0.0)
        cells.append(frame[s] + shift)
    cells.append(jnp.zeros((8, AT), f32))
    parts = []
    for half in (cells[:5], cells[5:]):
        parts += [t.astype(f32) for t in split3(jnp.concatenate(half, axis=1))]
    return jnp.concatenate(parts, axis=0).astype(bf16)


def geometry(gathered, idx, own, cnt):
    low = gathered[0:8] + gathered[8:16] + gathered[16:24]
    high = gathered[24:32] + gathered[32:40] + gathered[40:48]
    pos = jnp.where(idx >= HALF, high, low)
    rel = jnp.where(rowid((8, E)) < 3, pos - jnp.concatenate([own] * NB, axis=1), 0.0)
    kind = pos[3:4]
    dist = jnp.sqrt(colsum(rel * rel) + 0.25)
    inv = 1.0 / dist
    unit = rel * inv
    freq = (rowid((8, 1)) + 1).astype(f32) * (math.pi / CUT)
    arg = dist * freq
    live = jnp.concatenate([jnp.where(n < cnt, 1.0, 0.0) for n in range(NB)], axis=1)
    basis = jnp.sin(arg) / arg
    slope = (jnp.cos(arg) - basis) * (inv * live)
    return basis * live, slope, unit, inv, kind


def chain(db, du, slope, unit, inv):
    return du * inv + unit * (colsum(db * slope) - inv * colsum(du * unit))


def kind_rows(kind):
    return jnp.where(rowid((8, AT)).astype(f32) == kind, 1.0, 0.0).astype(bf16)


def embed_cols(embed8, kind):
    oh = kind_rows(kind)
    hi, mid, lo = split3(embed8)
    return dot(hi, oh, TN) + dot(mid, oh, TN) + dot(lo, oh, TN)


def first_sums(basis, unit, kind):
    sums = [jnp.zeros((32, AT), f32) for _ in range(NS)]
    for n in range(NB):
        sl = slice(n * AT, (n + 1) * AT)
        b, u, k = basis[:, sl], unit[:, sl], kind[:, sl]
        z = jnp.concatenate([b, b * u[0:1], b * u[1:2], b * u[2:3]], axis=0)
        for s in range(NS):
            sums[s] = sums[s] + jnp.where(k == float(s), z, 0.0)
    return [jnp.concatenate([t[8 * p : 8 * p + 8] for t in sums], axis=0) for p in range(4)]


def pair_rows(radial, embed8):
    return jnp.concatenate([radial * embed8[s : s + 1] for s in range(NS)], axis=0)


def layer_one(sums, own_kind, radial0, radial1, mix0, mix1, embed8):
    re0, re1 = pair_rows(radial0, embed8), pair_rows(radial1, embed8)
    m0 = dot3(re0, sums[0], TN) * NORM
    m1 = dot3(re1, jnp.concatenate(sums[1:], axis=1), TN) * NORM
    mx = [m1[:, p * AT : (p + 1) * AT] for p in range(3)]
    sq = mx[0] * mx[0] + mx[1] * mx[1] + mx[2] * mx[2]
    act, slope = silu_pair(dot3(mix0, m0, TN) + dot3(mix1, sq, TN))
    return embed_cols(embed8, own_kind) + act, slope, m1


def layer_one_back(grad, slope, m1, radial0, radial1, mix0, mix1, embed8):
    re0, re1 = pair_rows(radial0, embed8), pair_rows(radial1, embed8)
    dpre = grad * slope
    d0 = dot3(mix0, dpre, NN) * NORM
    dsq = dot3(mix1, dpre, NN) * (2.0 * NORM)
    d1 = m1 * jnp.concatenate([dsq] * 3, axis=1)
    a0 = dot3(re0, d0, NN)
    a1 = dot3(re1, d1, NN)
    return [a0] + [a1[:, p * AT : (p + 1) * AT] for p in range(3)]


def first_sums_back(n, sums, basis, unit, kind):
    z = []
    for t in sums:
        got = jnp.zeros((8, AT), f32)
        for s in range(NS):
            got = jnp.where(kind == float(s), t[8 * s : 8 * s + 8], got)
        z.append(got)
    db = z[0] + z[1] * unit[0:1] + z[2] * unit[1:2] + z[3] * unit[2:3]
    du = [colsum(basis * t) for t in z[1:]]
    return db, jnp.concatenate(du + [jnp.zeros((5, AT), f32)], axis=0)


def radial_left(radial0, radial1):
    r = jnp.concatenate([radial0, radial1], axis=1)
    hi, lo = split2(r)
    hi, lo = hi.astype(f32), lo.astype(f32)
    return jnp.concatenate([hi, hi, lo, jnp.zeros_like(hi)], axis=0).T.astype(bf16)


def basis_right(b):
    hi, lo = split2(b)
    hi, lo = hi.astype(f32), lo.astype(f32)
    return jnp.concatenate([hi, lo, hi, jnp.zeros_like(hi)], axis=0).astype(bf16)


def second_slot(folded, oh, idx_row, left, b):
    both = dot(folded, oh, NN)
    g = jnp.where(idx_row >= HALF, both[C:], both[:C])
    return g, dot(left, basis_right(b), NN)


def second_slot_back(g, w, idx_row, unit, d0, d1, rhi, rstack):
    w0, w1 = w[:C], w[C:]
    ux, uy, uz = unit[0:1], unit[1:2], unit[2:3]
    p = d1[0] * ux + d1[1] * uy + d1[2] * uz
    dg = w0 * d0 + w1 * p
    xh, xl = split2(jnp.concatenate([g * d0, g * p], axis=0))
    both = dot(rstack, xh, NN)
    db = both[:8] + both[8:] + dot(rhi, xl, NN)
    t = w1 * g
    du = [colsum(t * d) for d in d1]
    du = jnp.concatenate(du + [jnp.zeros((5, AT), f32)], axis=0)
    far = idx_row >= HALF
    dgm = jnp.concatenate([jnp.where(far, 0.0, dg), jnp.where(far, dg, 0.0)], axis=0)
    return dgm, db, du


def trig8(pos_row, origin, length):
    theta = (pos_row + origin) * (2.0 * math.pi / length)
    arg = theta * (rowid((8, 1)) + 1).astype(f32)
    return jnp.cos(arg), jnp.sin(arg)


def phases(pos, ox, oy, lx, ly, cq):
    c1, s1 = trig8(pos[0:1], ox, lx)
    c2, s2 = trig8(pos[1:2], oy, ly)
    c3, s3 = trig8(pos[2:3], 0.0, HEIGHT)
    cos, sin = [], []
    for m in range(8):
        a, b = c1[m : m + 1], s1[m : m + 1]
        cc, ss, sc, cs = a * c2, b * s2, b * c2, a * s2
        cos += [cc - ss, cc + ss]
        sin += [sc + cs, sc - cs]
    gap = [jnp.zeros((48, AT), f32)]
    plane = jnp.concatenate(cos + sin + [c1, c2] + gap + [s1, s2] + gap, axis=0)
    third = [jnp.where(rowid((2 * cq, AT)) < cq, 1.0, 0.0)]
    for m in range(8):
        third.append(jnp.where(rowid((2 * cq, AT)) < cq, c3[m : m + 1], s3[m : m + 1]))
    return plane, jnp.concatenate(third, axis=0)


def wave_cols(waves):
    k1, k2, k3 = waves[0:1], waves[1:2], waves[2:3]
    flip = (k1 < 0) | ((k1 == 0) & (k2 < 0))
    k1, k2, k3 = (jnp.where(flip, -k, k) for k in (k1, k2, k3))
    main = (k1 - 1) * 16 + jnp.where(k2 > 0, k2 - 1, 7 - k2)
    col = jnp.where(k1 == 0, 135 + k2, jnp.where(k2 == 0, 127 + k1, main))
    return col, k3


def count_part(col, k3, kappa):
    oh = jnp.where(rowid((256, AT)) == col, 1.0, 0.0).astype(bf16)
    r = rowid((8, AT))
    want = jnp.where(r == 0, kappa, jnp.where(r == 1, -kappa, 99))
    return dot(jnp.where(k3 == want, 1.0, 0.0).astype(bf16), oh, NT)


def col_numbers():
    lane = laneid((1, 256))
    low = (lane & 7) + 1
    k1 = jnp.where(lane < 128, (lane >> 4) + 1, jnp.where(lane < 136, low, 0))
    k2 = jnp.where(lane < 128, jnp.where((lane & 15) < 8, low, -low), jnp.where(lane < 136, 0, low))
    k2 = jnp.where(lane < 144, k2, 0)
    return k1.astype(f32), k2.astype(f32)


def widen(x):
    main, rest = x[:, :128], x[:, 128:]
    rest = jnp.where(laneid(rest.shape) < 64, rest, swap_lanes(rest))
    return jnp.concatenate([main, main, rest], axis=1)


def weights(count, kappa, lx, ly):
    k1, k2 = col_numbers()
    kz = kappa.astype(f32)
    wx, wy, wz = 2.0 * math.pi * k1 / lx, 2.0 * math.pi * k2 / ly, 2.0 * math.pi * kz / HEIGHT
    sq = wx * wx + wy * wy + wz * wz
    green = jnp.exp(-0.5 * sq) / (sq + 0.25)
    plus = count[0:1] * green
    minus = jnp.where(kappa == 0, 0.0, count[1:2] * green)
    return widen(plus + minus), widen(plus - minus)


def turn(t, sign):
    rest = t[:, 256:]
    swapped = swap_lanes(rest)
    rest = jnp.where(laneid(rest.shape) < 64, sign * swapped, -sign * swapped)
    return jnp.concatenate([sign * t[:, 128:256], -sign * t[:, :128], rest], axis=1)


def weigh(t, sigma, delta):
    cq = t.shape[0] // 2
    sign = jnp.where(rowid((2 * cq, 1)) < cq, -1.0, 1.0)
    return sigma * t + delta * turn(swap_rows(t), sign)


def fold_left(v, lx, ly):
    k1, k2 = col_numbers()
    kx, ky = widen(k1) * (2.0 * math.pi / lx), widen(k2) * (2.0 * math.pi / ly)
    t = turn(v, 1.0)
    return jnp.concatenate([v, kx * t, ky * t], axis=0)


def fold_cell(u, third, q):
    cq = q.shape[0]
    rows = KZ * 2 * cq
    zero = jnp.zeros((2 * cq, AT), f32)
    pot, gx, gy, gz = zero, zero, zero, zero
    for k in range(KZ):
        at = slice(k * 2 * cq, (k + 1) * 2 * cq)
        t, part = third[at], u[at]
        pot = pot + t * part
        gx = gx + t * u[rows:][at]
        gy = gy + t * u[2 * rows :][at]
        if k:
            gz = gz + swap_rows(t) * (part * (2.0 * math.pi * k / HEIGHT))
    qq = jnp.concatenate([q, q], axis=0)
    sign = jnp.where(rowid((2 * cq, 1)) < cq, -1.0, 1.0)
    rows = [pot[:cq] + pot[cq:], colsum(qq * gx), colsum(qq * gy), colsum(qq * gz * sign)]
    return jnp.concatenate(rows + [jnp.zeros((1, AT), f32)], axis=0)


def kernel(
    gx_n,
    gy_n,
    pos_ref,
    kind_ref,
    nbr_ref,
    cnt_ref,
    emb_ref,
    rad_ref,
    mix_ref,
    rh_ref,
    ro_ref,
    cm_ref,
    wave_ref,
    force_ref,
    site_ref,
    pfr,
    prow,
    hfr,
    oht,
    gfold,
    g_s,
    w_s,
    dgm_s,
    drel_s,
    basis_s,
    slope_s,
    unit_s,
    misc_s,
    m_s,
    ah,
    al,
    tr,
    t_s,
    q_send,
    q_recv,
    t_send,
    t_recv,
    v_send,
    v_all,
    b_send,
    b_recv,
    g_send,
    g_recv,
    f_send,
    f_recv,
    halo_s,
    halo_r,
    row_s,
    row_r,
    red_s,
    red_r,
    bc_s,
    bc_r,
):
    mx, my = lax.axis_index("gx"), lax.axis_index("gy")
    cq = cm_ref.shape[1] // gx_n
    lx, ly = CELL * gx_n, CELL * gy_n
    atoms_all = AT * gx_n * gy_n
    scale = 1.0 / math.sqrt(wave_ref.shape[1] * cm_ref.shape[1] * atoms_all)

    def cell(da, db):
        return lax.rem(mx + da + gx_n, gx_n), lax.rem(my + db + gy_n, gy_n)

    around = [(da, db) for da in (-1, 0, 1) for db in (-1, 0, 1) if (da, db) != (0, 0)]

    def remote(src, dst, ssem, rsem, dev):
        return pltpu.make_async_remote_copy(
            src_ref=src,
            dst_ref=dst,
            send_sem=ssem,
            recv_sem=rsem,
            device_id=dev,
            device_id_type=MESH,
        )

    def halo(stage, src_of, dst):
        copies = []
        for da, db in around:
            here, there = 3 * (da + 1) + db + 1, 3 * (1 - da) + 1 - db
            copies.append(
                remote(
                    src_of(here),
                    dst.at[there],
                    halo_s.at[stage, here],
                    halo_r.at[stage, there],
                    cell(da, db),
                )
            )
            copies[-1].start()
        return copies

    pending = []

    barrier = pltpu.get_barrier_semaphore()
    mates = [cell(d, 0) for d in range(1, gx_n)] + [cell(0, d) for d in range(1, gy_n)]
    mates += [cell(da, db) for da, db in around if da and db]
    for dev in mates:
        pl.semaphore_signal(barrier, inc=1, device_id=dev, device_id_type=MESH)

    row = rowid((8, AT))
    own = jnp.where(row == 3, kind_ref[0].astype(f32), 0.0)
    for p in range(3):
        own = jnp.where(row == p, pos_ref[0, 0, p : p + 1, :], own)
    pfr[4] = own
    prow[0] = own
    pl.semaphore_wait(barrier, len(mates))

    copies = halo(0, lambda here: pfr.at[4], pfr)
    row_pos = [
        remote(prow.at[0], prow.at[d], row_s.at[0, d], row_r.at[0, d], cell(d, 0))
        for d in range(1, gx_n)
    ]
    for c in row_pos:
        c.start()
    pending += copies + row_pos

    def slot(n):
        return pl.ds(pl.multiple_of(n * AT, AT), AT)

    def hot(n, _):
        oht[:, slot(n)] = one_hot(nbr_ref[pl.ds(n, 1), :])
        return 0

    lax.fori_loop(0, NB, hot, 0)
    embed8 = jnp.zeros((8, C), f32)
    for s in range(NS):
        embed8 = jnp.where(rowid((8, C)) == s, emb_ref[s : s + 1, :], embed8)
    idx = jnp.concatenate([nbr_ref[n : n + 1, :] for n in range(NB)], axis=1)
    for c in copies:
        c.wait_recv()

    gathered = dot(pos_table([pfr[s] for s in range(9)]), oht[...], NN)
    basis, slope, unit, inv, kind = geometry(gathered, idx, own, cnt_ref[0])
    basis_s[...] = basis
    slope_s[...] = slope
    unit_s[...] = unit
    misc_s[0:1] = inv
    misc_s[1:2] = kind
    layer = (rad_ref[0, 0], rad_ref[0, 1], mix_ref[0, 0], mix_ref[0, 1], embed8)
    hidden, slope1, m1_first = layer_one(first_sums(basis, unit, kind), own[3:4], *layer)
    hfr[4] = hidden.astype(bf16)
    copies = halo(1, lambda here: hfr.at[4], hfr)
    pending += copies

    for c in row_pos:
        c.wait_recv()

    def phase(d, _):
        source = lax.rem(mx - d + gx_n, gx_n)
        plane, third = phases(
            prow[d], source.astype(f32) * CELL, my.astype(f32) * CELL, lx, ly, cq
        )
        hi, lo = split2(plane)
        ah[d] = hi
        al[d] = lo
        tr[d] = third
        return 0

    lax.fori_loop(0, gx_n, phase, 0)
    owners = [k * gy_n // KZ for k in range(KZ)]
    kappa = (my * KZ + gy_n - 1) // gy_n
    owning = (kappa < KZ) & ((kappa * gy_n) // KZ == my)
    kappa = jnp.minimum(kappa, KZ - 1)

    def count(s, total):
        col, k3 = wave_cols(wave_ref[:, slot(s)])
        return total + count_part(col, k3, kappa)

    counted = lax.fori_loop(0, wave_ref.shape[1] // AT, count, jnp.zeros((8, AT), f32))
    sigma, delta = weights(counted, kappa, lx, ly)
    left = radial_left(rad_ref[1, 0], rad_ref[1, 1])
    for c in copies:
        c.wait_recv()

    for s in range(9):
        part = slice(0, C) if s < 5 else slice(C, 2 * C)
        gfold[part, (s % 5) * AT : (s % 5 + 1) * AT] = hfr[s]
    gfold[C:, 4 * AT :] = jnp.zeros((C, AT), bf16)
    m_s[...] = jnp.zeros_like(m_s)

    def forward(n, _):
        g, w = second_slot(
            gfold[...], oht[:, slot(n)], nbr_ref[pl.ds(n, 1), :], left, basis_s[:, slot(n)]
        )
        g_s[n] = g.astype(bf16)
        w_s[n] = w
        u = unit_s[:, slot(n)]
        m_s[0] += w[:C] * g
        t = w[C:] * g
        for p in range(3):
            m_s[1 + p] += t * u[p : p + 1]
        return 0

    lax.fori_loop(0, NB, forward, 0)
    m1 = [m_s[1 + p] * NORM for p in range(3)]
    sq = m1[0] * m1[0] + m1[1] * m1[1] + m1[2] * m1[2]
    act, slope2 = silu_pair(
        dot3(mix_ref[1, 0], m_s[0] * NORM, TN) + dot3(mix_ref[1, 1], sq, TN)
    )
    h2 = hfr[4].astype(f32) + act
    q = dot3(cm_ref[...], h2, TN)
    for p in range(gx_n):
        q_send[p] = jnp.concatenate([q[cq * p : cq * p + cq]] * 2, axis=0)
    q_recv[0] = q_send[mx]
    copies = []
    for d in range(1, gx_n):
        dev = cell(d, 0)
        copies.append(
            remote(q_send.at[dev[0]], q_recv.at[d], row_s.at[1, d], row_r.at[1, d], dev)
        )
        copies[-1].start()
    pending += copies
    r, rs = silu_pair(dot3(rh_ref[...], h2, TN))
    ro8 = jnp.broadcast_to(ro_ref[...], (8, C))
    energy = dot3(ro8, r, NN)[0:1]
    dread = dot3(rh_ref[...] * ro_ref[...], rs, NN)
    for c in copies:
        c.wait_recv()

    t_s[...] = jnp.zeros_like(t_s)

    def gather_terms(d, _):
        qh, ql = split2(tr[d] * jnp.concatenate([q_recv[d]] * KZ, axis=0))
        t_s[...] += dot(qh, ah[d], NT) + dot(ql, ah[d], NT) + dot(qh, al[d], NT)
        return 0

    lax.fori_loop(0, gx_n, gather_terms, 0)
    rows = 2 * cq
    for k in range(KZ):
        t_send[k] = t_s[k * rows : (k + 1) * rows, :]
    to_owner = []
    for k in range(KZ):
        to_owner.append(
            remote(t_send.at[k], t_recv.at[my], red_s.at[k], red_r.at[my], (mx, owners[k]))
        )
        pl.when(my != owners[k])(to_owner[-1].start)

    spread = [
        remote(v_send, v_all.at[kappa], bc_s.at[d], bc_r.at[kappa], cell(0, d))
        for d in range(1, gy_n)
    ]

    @pl.when(owning)
    def _():
        t_recv[my] = t_send[kappa]
        for d in range(1, gy_n):
            src = lax.rem(my + d, gy_n)
            remote(
                t_send.at[0], t_recv.at[src], red_s.at[0], red_r.at[src], (mx, src)
            ).wait_recv()
        total = t_recv[0]
        for j in range(1, gy_n):
            total = total + t_recv[j]
        v = weigh(total, sigma, delta)
        v_send[...] = v
        v_all[kappa] = v
        for c in spread:
            c.start()

    for k in range(KZ):
        arrive = remote(v_send, v_all.at[k], bc_s.at[0], bc_r.at[k], (mx, owners[k]))
        pl.when(my != owners[k])(arrive.wait_recv)

    lh, ll = split2(
        fold_left(jnp.concatenate([v_all[k] for k in range(KZ)], axis=0), lx, ly)
    )

    def back(d):
        dev = cell(-d, 0)
        return remote(b_send.at[d], b_recv.at[mx], row_s.at[2, d], row_r.at[2, d], dev)

    def fold(step, _):
        d = lax.rem(step, gx_n)
        u = dot(lh, ah[d], NN) + dot(ll, ah[d], NN) + dot(lh, al[d], NN)
        b_send[d] = fold_cell(u, tr[d], q_recv[d, :cq])

        @pl.when(d > 0)
        def _():
            back(d).start()

        return 0

    lax.fori_loop(1, gx_n + 1, fold, 0)
    b_recv[mx] = b_send[0]
    for d in range(1, gx_n):
        src = lax.rem(mx + d, gx_n)
        remote(
            b_send.at[d], b_recv.at[src], row_s.at[2, d], row_r.at[2, d], (src, my)
        ).wait_recv()
    pot = jnp.concatenate([b_recv[p, :cq] for p in range(gx_n)], axis=0)
    long_range = b_recv[0]
    for p in range(1, gx_n):
        long_range = long_range + b_recv[p]
    site_ref[0] = energy + scale * colsum(q * pot)

    dh = dread + dot3(cm_ref[...], pot * (2.0 * scale), NN)
    dpre = dh * slope2
    d0 = dot3(mix_ref[1, 0], dpre, NN) * NORM
    dsq = dot3(mix_ref[1, 1], dpre, NN) * (2.0 * NORM)
    m_s[0] = d0
    for p in range(3):
        m_s[1 + p] = m1[p] * dsq
    rhi, rlo = split2(jnp.concatenate([rad_ref[1, 0], rad_ref[1, 1]], axis=1))
    rstack = jnp.concatenate([rhi.astype(f32), rlo.astype(f32)], axis=0).astype(bf16)

    def backward(n, _):
        u = unit_s[:, slot(n)]
        dgm, db, du = second_slot_back(
            g_s[n].astype(f32),
            w_s[n],
            nbr_ref[pl.ds(n, 1), :],
            u,
            m_s[0],
            [m_s[1], m_s[2], m_s[3]],
            rhi,
            rstack,
        )
        dgm_s[:, slot(n)] = dgm.astype(bf16)
        drel_s[:, slot(n)] = chain(db, du, slope_s[:, slot(n)], u, misc_s[0:1, slot(n)])
        return 0

    lax.fori_loop(0, NB, backward, 0)
    cells = dot(dgm_s[...], oht[...], NT)
    for s in range(9):
        part = cells[:C] if s < 5 else cells[C:]
        g_send[s] = part[:, (s % 5) * AT : (s % 5 + 1) * AT].astype(bf16)
    copies = halo(2, lambda here: g_send.at[here], g_recv)
    pending += copies
    grad = dh + cells[:C, 4 * AT :]
    for c in copies:
        c.wait_recv()
    for s in range(9):
        if s != 4:
            grad = grad + g_recv[s].astype(f32)

    sums = layer_one_back(grad, slope1, m1_first, *layer)
    own_grad = jnp.zeros((8, AT), f32)
    drels = []
    for n in range(NB):
        sl = slice(n * AT, (n + 1) * AT)
        b, u = basis_s[:, sl], unit_s[:, sl]
        db, du = first_sums_back(n, sums, b, u, misc_s[1:2, sl])
        drel = drel_s[:, sl] + chain(db, du, slope_s[:, sl], u, misc_s[0:1, sl])
        own_grad = own_grad - drel
        drels.append(drel)
    terms = [t.astype(f32) for t in split3(jnp.concatenate(drels, axis=1))]
    far = idx >= HALF
    terms = [jnp.where(far, 0.0, t) for t in terms] + [jnp.where(far, t, 0.0) for t in terms]
    spots = dot(jnp.concatenate(terms, axis=0).astype(bf16), oht[...], NT)
    spots = [spots[:8] + spots[8:16] + spots[16:24], spots[24:32] + spots[32:40] + spots[40:48]]
    for s in range(9):
        f_send[s] = spots[s // 5][:, (s % 5) * AT : (s % 5 + 1) * AT]
    copies = halo(3, lambda here: f_send.at[here], f_recv)
    pending += copies
    total = own_grad + f_send[4]
    for c in copies:
        c.wait_recv()
    for s in range(9):
        if s != 4:
            total = total + f_recv[s]
    force_ref[0, 0] = -(total[:3] + (2.0 * scale) * long_range[cq : cq + 3])

    for c in pending:
        c.wait_send()
    for k in range(KZ):
        pl.when(my != owners[k])(to_owner[k].wait_send)

    @pl.when(owning)
    def _():
        for c in spread:
            c.wait_send()

    for d in range(1, gx_n):
        back(d).wait_send()


def per_device(
    positions,
    species,
    neighbours,
    counts,
    species_embed,
    radial,
    mixing,
    read_hidden,
    read_out,
    charge_map,
    wavevectors,
):
    gx_n, gy_n = lax.axis_size("gx"), lax.axis_size("gy")
    rows = 2 * (charge_map.shape[1] // gx_n)
    vmem = pltpu.VMEM
    sem = pltpu.SemaphoreType.DMA
    scratch = [
        vmem((9, 8, AT), f32),
        vmem((gx_n, 8, AT), f32),
        vmem((9, C, AT), bf16),
        vmem((HALF, E), bf16),
        vmem((2 * C, HALF), bf16),
        vmem((NB, C, AT), bf16),
        vmem((NB, 2 * C, AT), f32),
        vmem((2 * C, E), bf16),
        vmem((8, E), f32),
        vmem((8, E), f32),
        vmem((8, E), f32),
        vmem((8, E), f32),
        vmem((8, E), f32),
        vmem((4, C, AT), f32),
        vmem((gx_n, LANES, AT), bf16),
        vmem((gx_n, LANES, AT), bf16),
        vmem((gx_n, KZ * rows, AT), f32),
        vmem((KZ * rows, LANES), f32),
        vmem((gx_n, rows, AT), f32),
        vmem((gx_n, rows, AT), f32),
        vmem((KZ, rows, LANES), f32),
        vmem((gy_n, rows, LANES), f32),
        vmem((rows, LANES), f32),
        vmem((KZ, rows, LANES), f32),
        vmem((gx_n, 8, AT), f32),
        vmem((gx_n, 8, AT), f32),
        vmem((9, C, AT), bf16),
        vmem((9, C, AT), bf16),
        vmem((9, 8, AT), f32),
        vmem((9, 8, AT), f32),
        sem((4, 9)),
        sem((4, 9)),
        sem((3, gx_n)),
        sem((3, gx_n)),
        sem((KZ,)),
        sem((gy_n,)),
        sem((gy_n,)),
        sem((KZ,)),
    ]
    return pl.pallas_call(
        functools.partial(kernel, gx_n, gy_n),
        out_shape=(
            jax.ShapeDtypeStruct((1, 1, 3, AT), f32),
            jax.ShapeDtypeStruct((1, 1, AT), f32),
        ),
        in_specs=[pl.BlockSpec(memory_space=pltpu.VMEM)] * 11,
        out_specs=(pl.BlockSpec(memory_space=pltpu.VMEM),) * 2,
        scratch_shapes=scratch,
        compiler_params=pltpu.CompilerParams(
            collective_id=0, has_side_effects=True, vmem_limit_bytes=60 * 1024 * 1024
        ),
    )(
        positions,
        species,
        neighbours[0, 0].T,
        counts,
        species_embed,
        radial,
        mixing,
        read_hidden,
        read_out[None],
        charge_map,
        wavevectors,
    )


def solution(mesh):
    in_specs = (
        P("gx", "gy", None, None),
        P("gx", "gy", None),
        P("gx", "gy", None, None),
        P("gx", "gy", None),
        P(),
        P(),
        P(),
        P(),
        P(),
        P(),
        P(),
    )
    out_specs = (P("gx", "gy", None, None), P("gx", "gy", None))
    return jax.shard_map(
        per_device, mesh=mesh, in_specs=in_specs, out_specs=out_specs, check_vma=False
    )
```

time: 664 us -> 92.4 us (0.14); the launches traced: 657 us -> 92.1 us
  waiting for transfers between devices: 272 us -> 0 us
  matrix products: 184 us -> 0 us
  Pallas kernels: 0 us -> 86.4 us
  local copies, waits for them, and re-layouts: 78.5 us -> 5.14 us
  other arithmetic: 68.7 us -> 0 us
  starting transfers between devices: 31.6 us -> 0 us
  between operations: 15.2 us -> 0.66 us
    psum x1 -> x0, waiting for transfers between devices: 256 us -> none  [per_device(): structure = lax.psum(partial_sf, ('gx', 'gy'))]
    dot_general x84 -> x0, matrix products: 184 us -> none  [the longest x6 27.5 us: interact(): jnp.einsum('anc,xan->xac', weight_one * source, unit_vec, precision=highest)]
    pallas_call x0 -> x1, Pallas kernels: none -> 86.4 us  [per_device(): pl.pallas_call(functools.partial(kernel, gx_n, gy_n), out_shape=(jax.Shap...]
    scatter-add x3 -> x0, other arithmetic: 52.1 us -> none  [the longest x2 34.7 us: interact(): relative = src_pos[:, neighbour_ids] - own_pos[:, :, None]]
    gather x7 -> x0, local copies, waits for them, and re-layouts: 33.7 us -> none  [the longest x4 24.7 us: interact(): source = h_src[neighbour_ids]]
    ppermute x16 -> x0, starting transfers between devices: 31.6 us -> none  [the longest x8 16.4 us: passed_along(): return lax.ppermute(block, axis, route)]
    ppermute x16 -> x0, waiting for transfers between devices: 15.6 us -> none  [the longest x4 7.53 us: with_halo(): lax.ppermute(lax.slice_in_dim(block, block.shape[dim] - width, None, axis...]
    slice x32 -> x0, local copies, waits for them, and re-layouts: 14.7 us -> none  [the longest x16 14.3 us: phase_pair(): wave_part[0][None, :]]
  transfers between devices with their start and end apart: 17 -> 0, of which waited for: 10 -> 0; matrix products, arithmetic and copies ran while one was open for 3% -> 0% of each run, Pallas kernels for 0% -> 0%
where the time goes in v1:
time: 92.4 us; the launch traced here: 92.1 us
  Pallas kernels  86.4 us (94%)
  local copies, waits for them, and re-layouts  5.14 us (6%)
    pallas_call x1, Pallas kernels, per_device(): pl.pallas_call(functools.partial(kernel, gx_n, gy_n), out_shape=(jax.Shap...  86.4 us
    unnamed x8, local copies, waits for them, and re-layouts  3.87 us

profile of v1, /device:TPU:1, one launch (start us, length us, event | category | flops | bytes accessed | tf_op | source)
XLA Modules:
  0.0 92.1 jit_solution(15872188594108265773)
XLA Ops:
  0.6 0.0 copy-start
  0.6 1.3 %copy.13.pos_ref = f32[1,1,3,256]{3,2,1,0:T(4,128)} copy(f32[1,1,3,256]{3,1,2,0:T(1,128)} %param.11) | data formatting | bytes 6144 | tf_op args[0]
  1.9 1.3 %copy.18 = s32[1,1,256,12]{2,3,1,0:T(8,128)} copy(s32[1,1,256,12]{2,1,3,0:T(1,128)} %param.13) | data formatting | bytes 24576
  3.2 0.0 copy-done
  3.2 0.7 copy.14.cm_ref
  3.9 86.4 %shard_map.122 = (f32[1,1,3,256]{3,2,1,0:T(4,128)}, f32[1,1,256]{2,1,0:T(1,128)}) custom-call(f32[1,1,3,256]{3,2,1,0:T(4,128)} %copy.13.pos_ref, s32[1,1,256]{2,1,0:T(1,128)} %kind_ref.1, s32[12,256]{1,0:T(8,128)} %bitcast.6, s32[1,1,256]{2,1,0:T(1,128)} %cnt_ref.1, f32[6,128]{1,0:T(8,128)} %emb_ref.1, f32[2,2,8,128]{3,2,1,0:T(8,128)} %rad_ref.1, ...), custom_call_target="tpu_custom_call" | custom-call | tf_op jit(solution)/shard_map/pallas_call | solution.py:748
  90.3 0.0 copy-start.1
  90.3 1.3 %copy.15 = f32[1,1,3,256]{3,1,2,0:T(1,128)} copy(f32[1,1,3,256]{3,2,1,0:T(4,128)} %get-tuple-element.2) | data formatting | bytes 6144 | tf_op jit(solution)/shard_map/pallas_call | solution.py:748
  91.6 0.0 copy-done.1
  91.6 0.6 copy.20
Async XLA Ops:
  0.6 2.6 %copy-start = (f32[128,64]{0,1:T(8,128)S(1)}, f32[128,64]{0,1:T(8,128)}, u32[]{:S(2)}) copy-start(f32[128,64]{0,1:T(8,128)} %param.20) | copy-start | bytes 98308
  90.3 1.3 %copy-start.1 = (f32[1,1,256]{2,1,0:T(1,128)S(1)}, f32[1,1,256]{2,1,0:T(1,128)}, u32[]{:S(2)}) copy-start(f32[1,1,256]{2,1,0:T(1,128)} %get-tuple-element.7) | copy-start | bytes 3076

commit v2 on v1

--- a/solution.py
+++ b/solution.py
@@ -17,6 +17,8 @@
 HALF = 1280
 KZ = 9
 LANES = 384
+DEPTH = 896
+UNROLL = 4
 NORM = 1.0 / math.sqrt(NB)
 
 
@@ -64,9 +66,13 @@
     return jnp.concatenate([x[h:], x[:h]], axis=0)
 
 
-def swap_lanes(x):
-    h = x.shape[1] // 2
-    return jnp.concatenate([x[:, h:], x[:, :h]], axis=1)
+def shift_lanes(x, by):
+    by = by % x.shape[1]
+    return jnp.concatenate([x[:, -by:], x[:, :-by]], axis=1)
+
+
+def swap_sixteens(x):
+    return jnp.where(laneid(x.shape) < 16, shift_lanes(x, -16), shift_lanes(x, 16))
 
 
 def colsum(x):
@@ -222,12 +228,39 @@
         cc, ss, sc, cs = a * c2, b * s2, b * c2, a * s2
         cos += [cc - ss, cc + ss]
         sin += [sc + cs, sc - cs]
-    gap = [jnp.zeros((48, AT), f32)]
-    plane = jnp.concatenate(cos + sin + [c1, c2] + gap + [s1, s2] + gap, axis=0)
+    main = jnp.concatenate(cos + sin, axis=0)
+    rest = jnp.concatenate([c1, c2, s1, s2], axis=0)
     third = [jnp.where(rowid((2 * cq, AT)) < cq, 1.0, 0.0)]
     for m in range(8):
         third.append(jnp.where(rowid((2 * cq, AT)) < cq, c3[m : m + 1], s3[m : m + 1]))
-    return plane, jnp.concatenate(third, axis=0)
+    return main, rest, jnp.concatenate(third, axis=0)
+
+
+def phase_rows(main, rest):
+    mh, ml = split2(main)
+    rh, rl = (t.astype(f32) for t in split2(rest))
+    tail = jnp.concatenate([rh, rh, rl, jnp.zeros_like(rh)], axis=0).astype(bf16)
+    return mh, ml, tail
+
+
+def structure_cell(third, q2, mh, ml, tail):
+    n = third.shape[0]
+    qh, ql = split2(third * jnp.concatenate([q2] * KZ, axis=0))
+    qq = jnp.concatenate([qh, ql], axis=0)
+    both = dot(qq, mh, NT)
+    return both[:n] + both[n:] + dot(qh, ml, NT), dot(qq, tail, NT)
+
+
+def join_rest(both):
+    n = both.shape[0] // 2
+    return both[:n] + both[n:] + shift_lanes(both[:n], -64)
+
+
+def fold_depth(left):
+    hi, lo = split2(left)
+    rh, rl = hi[:, 256:].astype(f32), lo[:, 256:].astype(f32)
+    tail = (rh + shift_lanes(rl, 32) + shift_lanes(rh, 64)).astype(bf16)
+    return jnp.concatenate([hi[:, :256], lo[:, :256], hi[:, :256], tail], axis=1)
 
 
 def wave_cols(waves):
@@ -251,13 +284,13 @@
     low = (lane & 7) + 1
     k1 = jnp.where(lane < 128, (lane >> 4) + 1, jnp.where(lane < 136, low, 0))
     k2 = jnp.where(lane < 128, jnp.where((lane & 15) < 8, low, -low), jnp.where(lane < 136, 0, low))
-    k2 = jnp.where(lane < 144, k2, 0)
+    k1, k2 = jnp.where(lane < 144, k1, 0), jnp.where(lane < 144, k2, 0)
     return k1.astype(f32), k2.astype(f32)
 
 
 def widen(x):
     main, rest = x[:, :128], x[:, 128:]
-    rest = jnp.where(laneid(rest.shape) < 64, rest, swap_lanes(rest))
+    rest = rest + shift_lanes(rest, 16)
     return jnp.concatenate([main, main, rest], axis=1)
 
 
@@ -274,8 +307,8 @@
 
 def turn(t, sign):
     rest = t[:, 256:]
-    swapped = swap_lanes(rest)
-    rest = jnp.where(laneid(rest.shape) < 64, sign * swapped, -sign * swapped)
+    swapped = swap_sixteens(rest)
+    rest = jnp.where(laneid(rest.shape) < 16, sign * swapped, -sign * swapped)
     return jnp.concatenate([sign * t[:, 128:256], -sign * t[:, :128], rest], axis=1)
 
 
@@ -341,10 +374,11 @@
     unit_s,
     misc_s,
     m_s,
-    ah,
-    al,
+    ph,
     tr,
     t_s,
+    u_s,
+    lk,
     q_send,
     q_recv,
     t_send,
@@ -367,15 +401,18 @@
     bc_r,
 ):
     mx, my = lax.axis_index("gx"), lax.axis_index("gy")
-    cq = cm_ref.shape[1] // gx_n
+    cq = cm_ref.shape[0] // gx_n
     lx, ly = CELL * gx_n, CELL * gy_n
     atoms_all = AT * gx_n * gy_n
-    scale = 1.0 / math.sqrt(wave_ref.shape[1] * cm_ref.shape[1] * atoms_all)
+    scale = 1.0 / math.sqrt(wave_ref.shape[1] * cm_ref.shape[0] * atoms_all)
 
     def cell(da, db):
         return lax.rem(mx + da + gx_n, gx_n), lax.rem(my + db + gy_n, gy_n)
 
     around = [(da, db) for da in (-1, 0, 1) for db in (-1, 0, 1) if (da, db) != (0, 0)]
+    around.sort(key=lambda t: -abs(t[0]) - abs(t[1]))
+    far_col = sorted(range(1, gy_n), key=lambda d: -min(d % 4, 4 - d % 4) - min(d // 4, 4 - d // 4))
+    far_row = sorted(range(1, gx_n), key=lambda d: -min(d, gx_n - d))
 
     def remote(src, dst, ssem, rsem, dev):
         return pltpu.make_async_remote_copy(
@@ -387,14 +424,14 @@
             device_id_type=MESH,
         )
 
-    def halo(stage, src_of, dst):
+    def halo(stage, src_of, dst_of, pick=None):
         copies = []
-        for da, db in around:
+        for da, db in around if pick is None else pick:
             here, there = 3 * (da + 1) + db + 1, 3 * (1 - da) + 1 - db
             copies.append(
                 remote(
                     src_of(here),
-                    dst.at[there],
+                    dst_of(there),
                     halo_s.at[stage, here],
                     halo_r.at[stage, there],
                     cell(da, db),
@@ -404,6 +441,7 @@
         return copies
 
     pending = []
+    pfr[...] = jnp.zeros_like(pfr)
 
     barrier = pltpu.get_barrier_semaphore()
     mates = [cell(d, 0) for d in range(1, gx_n)] + [cell(0, d) for d in range(1, gy_n)]
@@ -414,15 +452,15 @@
     row = rowid((8, AT))
     own = jnp.where(row == 3, kind_ref[0].astype(f32), 0.0)
     for p in range(3):
-        own = jnp.where(row == p, pos_ref[0, 0, p : p + 1, :], own)
+        own = jnp.where(row == p, pos_ref[p], own)
     pfr[4] = own
     prow[0] = own
     pl.semaphore_wait(barrier, len(mates))
 
-    copies = halo(0, lambda here: pfr.at[4], pfr)
+    copies = halo(0, lambda here: pfr.at[4, :4], lambda there: pfr.at[there, :4])
     row_pos = [
-        remote(prow.at[0], prow.at[d], row_s.at[0, d], row_r.at[0, d], cell(d, 0))
-        for d in range(1, gx_n)
+        remote(prow.at[0, :3], prow.at[d, :3], row_s.at[0, d], row_r.at[0, d], cell(d, 0))
+        for d in far_row
     ]
     for c in row_pos:
         c.start()
@@ -432,14 +470,14 @@
         return pl.ds(pl.multiple_of(n * AT, AT), AT)
 
     def hot(n, _):
-        oht[:, slot(n)] = one_hot(nbr_ref[pl.ds(n, 1), :])
+        oht[:, slot(n)] = one_hot(nbr_ref[n])
         return 0
 
     lax.fori_loop(0, NB, hot, 0)
     embed8 = jnp.zeros((8, C), f32)
     for s in range(NS):
         embed8 = jnp.where(rowid((8, C)) == s, emb_ref[s : s + 1, :], embed8)
-    idx = jnp.concatenate([nbr_ref[n : n + 1, :] for n in range(NB)], axis=1)
+    idx = jnp.concatenate([nbr_ref[n] for n in range(NB)], axis=1)
     for c in copies:
         c.wait_recv()
 
@@ -453,7 +491,7 @@
     layer = (rad_ref[0, 0], rad_ref[0, 1], mix_ref[0, 0], mix_ref[0, 1], embed8)
     hidden, slope1, m1_first = layer_one(first_sums(basis, unit, kind), own[3:4], *layer)
     hfr[4] = hidden.astype(bf16)
-    copies = halo(1, lambda here: hfr.at[4], hfr)
+    copies = halo(1, lambda here: hfr.at[4], lambda there: hfr.at[there])
     pending += copies
 
     for c in row_pos:
@@ -461,26 +499,33 @@
 
     def phase(d, _):
         source = lax.rem(mx - d + gx_n, gx_n)
-        plane, third = phases(
+        main, rest, third = phases(
             prow[d], source.astype(f32) * CELL, my.astype(f32) * CELL, lx, ly, cq
         )
-        hi, lo = split2(plane)
-        ah[d] = hi
-        al[d] = lo
+        mh, ml, tail = phase_rows(main, rest)
+        ph[d, 0:256] = mh
+        ph[d, 256:512] = mh
+        ph[d, 512:768] = ml
+        ph[d, 768:] = tail
         tr[d] = third
         return 0
 
-    lax.fori_loop(0, gx_n, phase, 0)
+    lax.fori_loop(0, gx_n, phase, 0, unroll=UNROLL)
     owners = [k * gy_n // KZ for k in range(KZ)]
-    kappa = (my * KZ + gy_n - 1) // gy_n
-    owning = (kappa < KZ) & ((kappa * gy_n) // KZ == my)
-    kappa = jnp.minimum(kappa, KZ - 1)
+
+    def owned(j):
+        k = (j * KZ + gy_n - 1) // gy_n
+        takes = (k < KZ) & ((k * gy_n) // KZ == j)
+        return jnp.minimum(k, KZ - 1), takes
+
+    kappa, owning = owned(my)
 
     def count(s, total):
         col, k3 = wave_cols(wave_ref[:, slot(s)])
         return total + count_part(col, k3, kappa)
 
-    counted = lax.fori_loop(0, wave_ref.shape[1] // AT, count, jnp.zeros((8, AT), f32))
+    counted = jnp.zeros((8, AT), f32)
+    counted = lax.fori_loop(0, wave_ref.shape[1] // AT, count, counted, unroll=UNROLL)
     sigma, delta = weights(counted, kappa, lx, ly)
     left = radial_left(rad_ref[1, 0], rad_ref[1, 1])
     for c in copies:
@@ -494,7 +539,7 @@
 
     def forward(n, _):
         g, w = second_slot(
-            gfold[...], oht[:, slot(n)], nbr_ref[pl.ds(n, 1), :], left, basis_s[:, slot(n)]
+            gfold[...], oht[:, slot(n)], nbr_ref[n], left, basis_s[:, slot(n)]
         )
         g_s[n] = g.astype(bf16)
         w_s[n] = w
@@ -505,53 +550,57 @@
             m_s[1 + p] += t * u[p : p + 1]
         return 0
 
-    lax.fori_loop(0, NB, forward, 0)
+    lax.fori_loop(0, NB, forward, 0, unroll=UNROLL)
     m1 = [m_s[1 + p] * NORM for p in range(3)]
     sq = m1[0] * m1[0] + m1[1] * m1[1] + m1[2] * m1[2]
     act, slope2 = silu_pair(
         dot3(mix_ref[1, 0], m_s[0] * NORM, TN) + dot3(mix_ref[1, 1], sq, TN)
     )
     h2 = hfr[4].astype(f32) + act
-    q = dot3(cm_ref[...], h2, TN)
+    q = dot3(cm_ref[...], h2, NN)
     for p in range(gx_n):
         q_send[p] = jnp.concatenate([q[cq * p : cq * p + cq]] * 2, axis=0)
     q_recv[0] = q_send[mx]
-    copies = []
-    for d in range(1, gx_n):
+    q_copies = {}
+    for d in far_row:
         dev = cell(d, 0)
-        copies.append(
-            remote(q_send.at[dev[0]], q_recv.at[d], row_s.at[1, d], row_r.at[1, d], dev)
+        q_copies[d] = remote(
+            q_send.at[dev[0], :cq], q_recv.at[d, :cq], row_s.at[1, d], row_r.at[1, d], dev
         )
-        copies[-1].start()
-    pending += copies
+        q_copies[d].start()
+    pending += q_copies.values()
     r, rs = silu_pair(dot3(rh_ref[...], h2, TN))
     ro8 = jnp.broadcast_to(ro_ref[...], (8, C))
     energy = dot3(ro8, r, NN)[0:1]
     dread = dot3(rh_ref[...] * ro_ref[...], rs, NN)
-    for c in copies:
-        c.wait_recv()
 
     t_s[...] = jnp.zeros_like(t_s)
-
-    def gather_terms(d, _):
-        qh, ql = split2(tr[d] * jnp.concatenate([q_recv[d]] * KZ, axis=0))
-        t_s[...] += dot(qh, ah[d], NT) + dot(ql, ah[d], NT) + dot(qh, al[d], NT)
-        return 0
-
-    lax.fori_loop(0, gx_n, gather_terms, 0)
+    u_s[...] = jnp.zeros_like(u_s)
+    near = [0] + far_row[::-1]
+    for at in range(0, gx_n, UNROLL):
+        for d in near[at : at + UNROLL]:
+            if d:
+                q_copies[d].wait_recv()
+        for d in near[at : at + UNROLL]:
+            q2 = jnp.concatenate([q_recv[d, :cq]] * 2, axis=0)
+            main, rest = structure_cell(tr[d], q2, ph[d, 0:256], ph[d, 512:768], ph[d, 768:])
+            t_s[...] += main
+            u_s[...] += rest
     rows = 2 * cq
+    rest = join_rest(u_s[...])
     for k in range(KZ):
-        t_send[k] = t_s[k * rows : (k + 1) * rows, :]
+        t_send[k, :, :256] = t_s[k * rows : (k + 1) * rows, :]
+        t_send[k, :, 256:] = rest[k * rows : (k + 1) * rows]
     to_owner = []
-    for k in range(KZ):
-        to_owner.append(
-            remote(t_send.at[k], t_recv.at[my], red_s.at[k], red_r.at[my], (mx, owners[k]))
-        )
-        pl.when(my != owners[k])(to_owner[-1].start)
+    for d in far_col:
+        dev = cell(0, d)
+        k, takes = owned(dev[1])
+        copy = remote(t_send.at[k], t_recv.at[my], red_s.at[d], red_r.at[my], dev)
+        to_owner.append((takes, copy))
+        pl.when(takes)(copy.start)
 
     spread = [
-        remote(v_send, v_all.at[kappa], bc_s.at[d], bc_r.at[kappa], cell(0, d))
-        for d in range(1, gy_n)
+        remote(v_send, v_all.at[kappa], bc_s.at[d], bc_r.at[kappa], cell(0, d)) for d in far_col
     ]
 
     @pl.when(owning)
@@ -560,7 +609,7 @@
         for d in range(1, gy_n):
             src = lax.rem(my + d, gy_n)
             remote(
-                t_send.at[0], t_recv.at[src], red_s.at[0], red_r.at[src], (mx, src)
+                t_send.at[0], t_recv.at[src], red_s.at[1], red_r.at[src], (mx, src)
             ).wait_recv()
         total = t_recv[0]
         for j in range(1, gy_n):
@@ -575,39 +624,39 @@
         arrive = remote(v_send, v_all.at[k], bc_s.at[0], bc_r.at[k], (mx, owners[k]))
         pl.when(my != owners[k])(arrive.wait_recv)
 
-    lh, ll = split2(
-        fold_left(jnp.concatenate([v_all[k] for k in range(KZ)], axis=0), lx, ly)
-    )
+    v = jnp.concatenate([v_all[k] for k in range(KZ)], axis=0)
+    lk[...] = fold_depth(fold_left(v, lx, ly))
 
     def back(d):
         dev = cell(-d, 0)
-        return remote(b_send.at[d], b_recv.at[mx], row_s.at[2, d], row_r.at[2, d], dev)
-
-    def fold(step, _):
-        d = lax.rem(step, gx_n)
-        u = dot(lh, ah[d], NN) + dot(ll, ah[d], NN) + dot(lh, al[d], NN)
-        b_send[d] = fold_cell(u, tr[d], q_recv[d, :cq])
-
-        @pl.when(d > 0)
-        def _():
-            back(d).start()
-
-        return 0
-
-    lax.fori_loop(1, gx_n + 1, fold, 0)
+        return remote(
+            b_send.at[d, : cq + 3], b_recv.at[mx, : cq + 3], row_s.at[2, d], row_r.at[2, d], dev
+        )
+
+    order = far_row + [0]
+    for at in range(0, gx_n, UNROLL):
+        for d in order[at : at + UNROLL]:
+            b_send[d] = fold_cell(dot(lk[...], ph[d], NN), tr[d], q_recv[d, :cq])
+        for d in order[at : at + UNROLL]:
+            if d:
+                back(d).start()
     b_recv[mx] = b_send[0]
     for d in range(1, gx_n):
         src = lax.rem(mx + d, gx_n)
         remote(
-            b_send.at[d], b_recv.at[src], row_s.at[2, d], row_r.at[2, d], (src, my)
+            b_send.at[d, : cq + 3],
+            b_recv.at[src, : cq + 3],
+            row_s.at[2, d],
+            row_r.at[2, d],
+            (src, my),
         ).wait_recv()
     pot = jnp.concatenate([b_recv[p, :cq] for p in range(gx_n)], axis=0)
-    long_range = b_recv[0]
+    long_range = b_recv[0, cq : cq + 3]
     for p in range(1, gx_n):
-        long_range = long_range + b_recv[p]
+        long_range = long_range + b_recv[p, cq : cq + 3]
     site_ref[0] = energy + scale * colsum(q * pot)
 
-    dh = dread + dot3(cm_ref[...], pot * (2.0 * scale), NN)
+    dh = dread + dot3(cm_ref[...], pot * (2.0 * scale), TN)
     dpre = dh * slope2
     d0 = dot3(mix_ref[1, 0], dpre, NN) * NORM
     dsq = dot3(mix_ref[1, 1], dpre, NN) * (2.0 * NORM)
@@ -622,7 +671,7 @@
         dgm, db, du = second_slot_back(
             g_s[n].astype(f32),
             w_s[n],
-            nbr_ref[pl.ds(n, 1), :],
+            nbr_ref[n],
             u,
             m_s[0],
             [m_s[1], m_s[2], m_s[3]],
@@ -633,14 +682,19 @@
         drel_s[:, slot(n)] = chain(db, du, slope_s[:, slot(n)], u, misc_s[0:1, slot(n)])
         return 0
 
-    lax.fori_loop(0, NB, backward, 0)
-    cells = dot(dgm_s[...], oht[...], NT)
-    for s in range(9):
-        part = cells[:C] if s < 5 else cells[C:]
-        g_send[s] = part[:, (s % 5) * AT : (s % 5 + 1) * AT].astype(bf16)
-    copies = halo(2, lambda here: g_send.at[here], g_recv)
+    lax.fori_loop(0, NB, backward, 0, unroll=UNROLL)
+    copies = []
+    for t in range(5):
+        part = dot(dgm_s[...], oht[t * AT : (t + 1) * AT, :], NT)
+        if t == 4:
+            grad = dh + part[:C]
+            break
+        for s, value in ((t, part[:C]), (t + 5, part[C:])):
+            g_send[s] = value.astype(bf16)
+            copies += halo(
+                2, lambda h: g_send.at[h], lambda h: g_recv.at[h], [(s // 3 - 1, s % 3 - 1)]
+            )
     pending += copies
-    grad = dh + cells[:C, 4 * AT :]
     for c in copies:
         c.wait_recv()
     for s in range(9):
@@ -660,24 +714,37 @@
     terms = [t.astype(f32) for t in split3(jnp.concatenate(drels, axis=1))]
     far = idx >= HALF
     terms = [jnp.where(far, 0.0, t) for t in terms] + [jnp.where(far, t, 0.0) for t in terms]
-    spots = dot(jnp.concatenate(terms, axis=0).astype(bf16), oht[...], NT)
-    spots = [spots[:8] + spots[8:16] + spots[16:24], spots[24:32] + spots[32:40] + spots[40:48]]
-    for s in range(9):
-        f_send[s] = spots[s // 5][:, (s % 5) * AT : (s % 5 + 1) * AT]
-    copies = halo(3, lambda here: f_send.at[here], f_recv)
+    terms = jnp.concatenate(terms, axis=0).astype(bf16)
+    copies = []
+    for t in range(5):
+        part = dot(terms, oht[t * AT : (t + 1) * AT, :], NT)
+        low = part[:8] + part[8:16] + part[16:24]
+        if t == 4:
+            total = own_grad + low
+            break
+        for s, value in ((t, low), (t + 5, part[24:32] + part[32:40] + part[40:48])):
+            f_send[s] = value
+            copies += halo(
+                3,
+                lambda h: f_send.at[h, :3],
+                lambda h: f_recv.at[h, :3],
+                [(s // 3 - 1, s % 3 - 1)],
+            )
     pending += copies
-    total = own_grad + f_send[4]
+    total = total[:3]
     for c in copies:
         c.wait_recv()
     for s in range(9):
         if s != 4:
-            total = total + f_recv[s]
-    force_ref[0, 0] = -(total[:3] + (2.0 * scale) * long_range[cq : cq + 3])
+            total = total + f_recv[s, :3]
+    total = -(total + (2.0 * scale) * long_range)
+    for p in range(3):
+        force_ref[p] = total[p : p + 1]
 
     for c in pending:
         c.wait_send()
-    for k in range(KZ):
-        pl.when(my != owners[k])(to_owner[k].wait_send)
+    for takes, copy in to_owner:
+        pl.when(takes)(copy.wait_send)
 
     @pl.when(owning)
     def _():
@@ -720,10 +787,11 @@
         vmem((8, E), f32),
         vmem((8, E), f32),
         vmem((4, C, AT), f32),
-        vmem((gx_n, LANES, AT), bf16),
-        vmem((gx_n, LANES, AT), bf16),
+        vmem((gx_n, DEPTH, AT), bf16),
         vmem((gx_n, KZ * rows, AT), f32),
-        vmem((KZ * rows, LANES), f32),
+        vmem((KZ * rows, 256), f32),
+        vmem((2 * KZ * rows, 128), f32),
+        vmem((3 * KZ * rows, DEPTH), bf16),
         vmem((gx_n, rows, AT), f32),
         vmem((gx_n, rows, AT), f32),
         vmem((KZ, rows, LANES), f32),
@@ -740,15 +808,15 @@
         sem((4, 9)),
         sem((3, gx_n)),
         sem((3, gx_n)),
-        sem((KZ,)),
+        sem((gy_n,)),
         sem((gy_n,)),
         sem((gy_n,)),
         sem((KZ,)),
     ]
-    return pl.pallas_call(
+    forces, site_energy = pl.pallas_call(
         functools.partial(kernel, gx_n, gy_n),
         out_shape=(
-            jax.ShapeDtypeStruct((1, 1, 3, AT), f32),
+            jax.ShapeDtypeStruct((3, 1, AT), f32),
             jax.ShapeDtypeStruct((1, 1, AT), f32),
         ),
         in_specs=[pl.BlockSpec(memory_space=pltpu.VMEM)] * 11,
@@ -758,18 +826,19 @@
             collective_id=0, has_side_effects=True, vmem_limit_bytes=60 * 1024 * 1024
         ),
     )(
-        positions,
+        jnp.transpose(positions[0], (1, 0, 2)),
         species,
-        neighbours[0, 0].T,
+        jnp.transpose(neighbours[0], (2, 0, 1)),
         counts,
         species_embed,
         radial,
         mixing,
         read_hidden,
         read_out[None],
-        charge_map,
+        charge_map.T,
         wavevectors,
     )
+    return jnp.transpose(forces, (1, 0, 2))[None], site_energy
 
 
 def solution(mesh):

time: 92.4 us -> 77.3 us (0.84)
  Pallas kernels: 86.4 us -> 74.7 us
  local copies, waits for them, and re-layouts: 5.14 us -> 1.87 us
    pallas_call x1, Pallas kernels: 86.4 us -> 74.7 us  [per_device(): pl.pallas_call(functools.partial(kernel, gx_n, gy_n), out_shape=(jax.Shap...]
    unnamed x8 -> x6, local copies, waits for them, and re-layouts: 3.87 us -> 1.87 us
    pallas_call x1 -> x0, local copies, waits for them, and re-layouts: 1.27 us -> none  [per_device(): pl.pallas_call(functools.partial(kernel, gx_n, gy_n), out_shape=(jax.Shap...]
where the time goes in v2:
time: 77.3 us; the launch traced here: 77.2 us
  Pallas kernels  74.7 us (97%)
  local copies, waits for them, and re-layouts  1.87 us (2%)
    pallas_call x1, Pallas kernels, per_device(): pl.pallas_call(functools.partial(kernel, gx_n, gy_n), out_shape=(jax.Shap...  74.7 us
    unnamed x6, local copies, waits for them, and re-layouts  1.87 us

profile of v2, /device:TPU:1, one launch (start us, length us, event | category | flops | bytes accessed | tf_op | source)
XLA Modules:
  0.0 77.2 jit_solution(17403727133876045529)
XLA Ops:
  0.6 74.7 %shard_map.122 = (f32[3,1,256]{2,1,0:T(1,128)}, f32[1,1,256]{2,1,0:T(1,128)}) custom-call(f32[3,1,256]{2,1,0:T(1,128)} %bitcast.11, s32[1,1,256]{2,1,0:T(1,128)} %kind_ref.1, s32[12,1,256]{2,1,0:T(1,128)} %bitcast.10, s32[1,1,256]{2,1,0:T(1,128)} %cnt_ref.1, f32[6,128]{1,0:T(8,128)} %emb_ref.1, f32[2,2,8,128]{3,2,1,0:T(8,128)} %rad_ref.1, ...), custom_call_target="tpu_custom_call" | custom-call | tf_op jit(solution)/shard_map/pallas_call | solution.py:816
  75.3 0.0 copy-start
  75.3 0.7 copy-done
  76.0 0.0 copy-start.1
  76.0 0.6 copy.16
  76.6 0.1 copy-done.1
  76.6 0.6 copy.17
Async XLA Ops:
  75.3 0.7 copy-start
  76.0 0.6 copy-start.1

commit v3 on v2

--- a/solution.py
+++ b/solution.py
@@ -20,6 +20,8 @@
 DEPTH = 896
 UNROLL = 4
 NORM = 1.0 / math.sqrt(NB)
+TILES = ((4, None), (1, 7), (3, 5), (0, 2), (6, 8))
+NEAR = 3 * AT
 
 
 def dot(a, b, dims):
@@ -44,6 +46,11 @@
     return dot(ah, bh, dims) + dot(ah, bl, dims) + dot(al, bh, dims)
 
 
+def dot3s(a, b):
+    bh, bl = split2(b)
+    return dot(a[0], bh, NN) + dot(a[0], bl, NN) + dot(a[1], bh, NN)
+
+
 def rowid(shape):
     return lax.broadcasted_iota(jnp.int32, shape, 0)
 
@@ -79,29 +86,40 @@
     return jnp.sum(x, axis=0, keepdims=True)
 
 
-def one_hot(idx_row):
-    f = jnp.where(idx_row >= HALF, idx_row - HALF, idx_row)
+def folded(idx_row):
+    which = idx_row >> 8
+    tile, far = jnp.zeros_like(idx_row), jnp.zeros_like(idx_row)
+    for t, pair in enumerate(TILES[1:], 1):
+        tile = jnp.where((which == pair[0]) | (which == pair[1]), t, tile)
+        far = jnp.where(which == pair[1], 1, far)
+    return tile * AT + (idx_row & (AT - 1)), far
+
+
+def one_hot(f):
     return jnp.where(rowid((HALF, AT)) == f, 1.0, 0.0).astype(bf16)
 
 
-def pos_table(frame):
-    cells = []
-    for s in range(9):
-        a, b = divmod(s, 3)
-        r = rowid((8, AT))
-        shift = jnp.where(r == 0, CELL * (a - 1), 0.0) + jnp.where(r == 1, CELL * (b - 1), 0.0)
-        cells.append(frame[s] + shift)
-    cells.append(jnp.zeros((8, AT), f32))
+def pos_table(frame, tiles):
     parts = []
-    for half in (cells[:5], cells[5:]):
-        parts += [t.astype(f32) for t in split3(jnp.concatenate(half, axis=1))]
+    for side in range(2):
+        cells = []
+        for pair in tiles:
+            s = pair[side]
+            if s is None:
+                cells.append(jnp.zeros((8, AT), f32))
+                continue
+            a, b = divmod(s, 3)
+            r = rowid((8, AT))
+            shift = jnp.where(r == 0, CELL * (a - 1), 0.0) + jnp.where(r == 1, CELL * (b - 1), 0.0)
+            cells.append(frame[s] + shift)
+        parts += [t.astype(f32) for t in split3(jnp.concatenate(cells, axis=1))]
     return jnp.concatenate(parts, axis=0).astype(bf16)
 
 
-def geometry(gathered, idx, own, cnt):
+def geometry(gathered, far, own, cnt):
     low = gathered[0:8] + gathered[8:16] + gathered[16:24]
     high = gathered[24:32] + gathered[32:40] + gathered[40:48]
-    pos = jnp.where(idx >= HALF, high, low)
+    pos = jnp.where(far > 0, high, low)
     rel = jnp.where(rowid((8, E)) < 3, pos - jnp.concatenate([own] * NB, axis=1), 0.0)
     kind = pos[3:4]
     dist = jnp.sqrt(colsum(rel * rel) + 0.25)
@@ -144,24 +162,22 @@
     return jnp.concatenate([radial * embed8[s : s + 1] for s in range(NS)], axis=0)
 
 
-def layer_one(sums, own_kind, radial0, radial1, mix0, mix1, embed8):
-    re0, re1 = pair_rows(radial0, embed8), pair_rows(radial1, embed8)
-    m0 = dot3(re0, sums[0], TN) * NORM
-    m1 = dot3(re1, jnp.concatenate(sums[1:], axis=1), TN) * NORM
+def layer_one(sums, initial, re0, re1, mix0, mix1):
+    m0 = dot3s(re0, sums[0]) * NORM
+    m1 = dot3s(re1, jnp.concatenate(sums[1:], axis=1)) * NORM
     mx = [m1[:, p * AT : (p + 1) * AT] for p in range(3)]
     sq = mx[0] * mx[0] + mx[1] * mx[1] + mx[2] * mx[2]
-    act, slope = silu_pair(dot3(mix0, m0, TN) + dot3(mix1, sq, TN))
-    return embed_cols(embed8, own_kind) + act, slope, m1
-
-
-def layer_one_back(grad, slope, m1, radial0, radial1, mix0, mix1, embed8):
-    re0, re1 = pair_rows(radial0, embed8), pair_rows(radial1, embed8)
+    act, slope = silu_pair(dot3s(mix0, m0) + dot3s(mix1, sq))
+    return initial + act, slope, m1
+
+
+def layer_one_back(grad, slope, m1, re0, re1, mix0, mix1):
     dpre = grad * slope
-    d0 = dot3(mix0, dpre, NN) * NORM
-    dsq = dot3(mix1, dpre, NN) * (2.0 * NORM)
+    d0 = dot3s(mix0, dpre) * NORM
+    dsq = dot3s(mix1, dpre) * (2.0 * NORM)
     d1 = m1 * jnp.concatenate([dsq] * 3, axis=1)
-    a0 = dot3(re0, d0, NN)
-    a1 = dot3(re1, d1, NN)
+    a0 = dot3s(re0, d0)
+    a1 = dot3s(re1, d1)
     return [a0] + [a1[:, p * AT : (p + 1) * AT] for p in range(3)]
 
 
@@ -190,13 +206,7 @@
     return jnp.concatenate([hi, lo, hi, jnp.zeros_like(hi)], axis=0).astype(bf16)
 
 
-def second_slot(folded, oh, idx_row, left, b):
-    both = dot(folded, oh, NN)
-    g = jnp.where(idx_row >= HALF, both[C:], both[:C])
-    return g, dot(left, basis_right(b), NN)
-
-
-def second_slot_back(g, w, idx_row, unit, d0, d1, rhi, rstack):
+def second_slot_back(g, w, far, unit, d0, d1, rhi, rstack):
     w0, w1 = w[:C], w[C:]
     ux, uy, uz = unit[0:1], unit[1:2], unit[2:3]
     p = d1[0] * ux + d1[1] * uy + d1[2] * uz
@@ -207,7 +217,7 @@
     t = w1 * g
     du = [colsum(t * d) for d in d1]
     du = jnp.concatenate(du + [jnp.zeros((5, AT), f32)], axis=0)
-    far = idx_row >= HALF
+    far = far > 0
     dgm = jnp.concatenate([jnp.where(far, 0.0, dg), jnp.where(far, dg, 0.0)], axis=0)
     return dgm, db, du
 
@@ -347,59 +357,18 @@
 def kernel(
     gx_n,
     gy_n,
-    pos_ref,
-    kind_ref,
-    nbr_ref,
-    cnt_ref,
-    emb_ref,
-    rad_ref,
-    mix_ref,
-    rh_ref,
-    ro_ref,
-    cm_ref,
-    wave_ref,
-    force_ref,
-    site_ref,
-    pfr,
-    prow,
-    hfr,
-    oht,
-    gfold,
-    g_s,
-    w_s,
-    dgm_s,
-    drel_s,
-    basis_s,
-    slope_s,
-    unit_s,
-    misc_s,
-    m_s,
-    ph,
-    tr,
-    t_s,
-    u_s,
-    lk,
-    q_send,
-    q_recv,
-    t_send,
-    t_recv,
-    v_send,
-    v_all,
-    b_send,
-    b_recv,
-    g_send,
-    g_recv,
-    f_send,
-    f_recv,
-    halo_s,
-    halo_r,
-    row_s,
-    row_r,
-    red_s,
-    red_r,
-    bc_s,
-    bc_r,
+    *refs,
 ):
+    arrays, (force_ref, site_ref), rest = refs[:11], refs[11:13], refs[13:]
+    kept, load_s, rest = rest[:11], rest[11], rest[12:]
+    pos_ref, kind_ref, nbr_ref, cnt_ref, emb_ref, rad_ref, mix_ref, rh_ref = kept[:8]
+    ro_ref, cm_ref, wave_ref = kept[8:]
+    (
+        pfr, prow, hfr, oht, half_s, fold_s, part_s, gp_s, gfold, g_s, w_s, dgm_s,
+        drel_s, basis_s, slope_s, unit_s, misc_s, m_s, ph, tr, t_s, u_s, lk, q_send,
+        q_recv, t_send, t_recv, v_send, v_all, b_send, b_recv, g_send, g_recv, f_send,
+        f_recv, halo_s, halo_r, row_s, row_r, red_s, red_r, bc_s, bc_r,
+    ) = rest
     mx, my = lax.axis_index("gx"), lax.axis_index("gy")
     cq = cm_ref.shape[0] // gx_n
     lx, ly = CELL * gx_n, CELL * gy_n
@@ -442,6 +411,9 @@
 
     pending = []
     pfr[...] = jnp.zeros_like(pfr)
+    loads = [
+        pltpu.make_async_copy(a, k, load_s.at[i]) for i, (a, k) in enumerate(zip(arrays, kept))
+    ]
 
     barrier = pltpu.get_barrier_semaphore()
     mates = [cell(d, 0) for d in range(1, gx_n)] + [cell(0, d) for d in range(1, gy_n)]
@@ -449,6 +421,10 @@
     for dev in mates:
         pl.semaphore_signal(barrier, inc=1, device_id=dev, device_id_type=MESH)
 
+    for c in loads:
+        c.start()
+    for c in loads[:2]:
+        c.wait()
     row = rowid((8, AT))
     own = jnp.where(row == 3, kind_ref[0].astype(f32), 0.0)
     for p in range(3):
@@ -465,34 +441,54 @@
     for c in row_pos:
         c.start()
     pending += copies + row_pos
+    for c in loads[2:]:
+        c.wait()
 
     def slot(n):
         return pl.ds(pl.multiple_of(n * AT, AT), AT)
 
     def hot(n, _):
-        oht[:, slot(n)] = one_hot(nbr_ref[n])
+        f, far = folded(nbr_ref[n])
+        fold_s[n] = f
+        half_s[n] = far
+        oht[:, slot(n)] = one_hot(f)
         return 0
 
     lax.fori_loop(0, NB, hot, 0)
     embed8 = jnp.zeros((8, C), f32)
     for s in range(NS):
         embed8 = jnp.where(rowid((8, C)) == s, emb_ref[s : s + 1, :], embed8)
-    idx = jnp.concatenate([nbr_ref[n] for n in range(NB)], axis=1)
-    for c in copies:
+    far = jnp.concatenate([half_s[n] for n in range(NB)], axis=1)
+    initial = embed_cols(embed8, own[3:4])
+    pairs = [pair_rows(rad_ref[0, p], embed8) for p in range(2)]
+    turned = [split2(m.T) for m in pairs + [mix_ref[0, 0], mix_ref[0, 1]]]
+    for c in copies[4:]:
         c.wait_recv()
-
-    gathered = dot(pos_table([pfr[s] for s in range(9)]), oht[...], NN)
-    basis, slope, unit, inv, kind = geometry(gathered, idx, own, cnt_ref[0])
+    gp_s[...] = dot(pos_table(pfr, TILES[:3]), oht[:NEAR, :], NN)
+    for c in copies[:4]:
+        c.wait_recv()
+
+    gathered = gp_s[...] + dot(pos_table(pfr, TILES[3:]), oht[NEAR:, :], NN)
+    basis, slope, unit, inv, kind = geometry(gathered, far, own, cnt_ref[0])
     basis_s[...] = basis
     slope_s[...] = slope
     unit_s[...] = unit
     misc_s[0:1] = inv
     misc_s[1:2] = kind
-    layer = (rad_ref[0, 0], rad_ref[0, 1], mix_ref[0, 0], mix_ref[0, 1], embed8)
-    hidden, slope1, m1_first = layer_one(first_sums(basis, unit, kind), own[3:4], *layer)
+    hidden, slope1, m1_first = layer_one(first_sums(basis, unit, kind), initial, *turned)
     hfr[4] = hidden.astype(bf16)
-    copies = halo(1, lambda here: hfr.at[4], lambda there: hfr.at[there])
-    pending += copies
+    side = 1 - 2 * lax.rem(mx, 2)
+    outer, inner = 3 * (1 - side), 3 * (1 + side)
+
+    def feature(src, dst, sem_at, dev):
+        return remote(hfr.at[src], hfr.at[dst], halo_s.at[1, sem_at], halo_r.at[1, dst], dev)
+
+    along_y = [feature(4, 4 - e, 4 + e, cell(0, e)) for e in (-1, 1)]
+    corners = [feature(4, inner + 1 - e, 1 + e, cell(-side, e)) for e in (-1, 1)]
+    along_x = [feature(4, 4 - 3 * e, 4 + 3 * e, cell(e, 0)) for e in (-1, 1)]
+    for c in along_y + corners + along_x:
+        c.start()
+    pending += along_y + corners + along_x
 
     for c in row_pos:
         c.wait_recv()
@@ -528,21 +524,44 @@
     counted = lax.fori_loop(0, wave_ref.shape[1] // AT, count, counted, unroll=UNROLL)
     sigma, delta = weights(counted, kappa, lx, ly)
     left = radial_left(rad_ref[1, 0], rad_ref[1, 1])
-    for c in copies:
+
+    def frame_tile(t):
+        for side, cell_at in enumerate(TILES[t]):
+            if cell_at is not None:
+                gfold[side * C : side * C + C, t * AT : (t + 1) * AT] = hfr[cell_at]
+
+    mix_turned = [split2(mix_ref[1, p].T) for p in range(2)]
+    cm_split, rh_turned = split2(cm_ref[...]), split2(rh_ref[...].T)
+    gfold[C:, :AT] = jnp.zeros((C, AT), bf16)
+    m_s[...] = jnp.zeros_like(m_s)
+    passed = []
+    for c, e in zip(along_y, (-1, 1)):
         c.wait_recv()
-
-    for s in range(9):
-        part = slice(0, C) if s < 5 else slice(C, 2 * C)
-        gfold[part, (s % 5) * AT : (s % 5 + 1) * AT] = hfr[s]
-    gfold[C:, 4 * AT :] = jnp.zeros((C, AT), bf16)
-    m_s[...] = jnp.zeros_like(m_s)
+        passed.append(feature(4 - e, outer + 1 - e, 7 + e, cell(side, 0)))
+        passed[-1].start()
+    pending += passed
+    for c in along_x:
+        c.wait_recv()
+    for t in range(3):
+        frame_tile(t)
+
+    def near_part(n, _):
+        part_s[n] = dot(gfold[:, :NEAR], oht[:NEAR, slot(n)], NN)
+        w_s[n] = dot(left, basis_right(basis_s[:, slot(n)]), NN)
+        return 0
+
+    lax.fori_loop(0, NB, near_part, 0, unroll=UNROLL)
+    for e in (-1, 1):
+        feature(4, outer + 1 + e, 1 + e, cell(0, e)).wait_recv()
+        feature(4, inner + 1 + e, 1 + e, cell(0, e)).wait_recv()
+    for t in range(3, 5):
+        frame_tile(t)
 
     def forward(n, _):
-        g, w = second_slot(
-            gfold[...], oht[:, slot(n)], nbr_ref[n], left, basis_s[:, slot(n)]
-        )
+        both = part_s[n] + dot(gfold[:, NEAR:], oht[NEAR:, slot(n)], NN)
+        g = jnp.where(half_s[n] > 0, both[C:], both[:C])
         g_s[n] = g.astype(bf16)
-        w_s[n] = w
+        w = w_s[n]
         u = unit_s[:, slot(n)]
         m_s[0] += w[:C] * g
         t = w[C:] * g
@@ -554,13 +573,13 @@
     m1 = [m_s[1 + p] * NORM for p in range(3)]
     sq = m1[0] * m1[0] + m1[1] * m1[1] + m1[2] * m1[2]
     act, slope2 = silu_pair(
-        dot3(mix_ref[1, 0], m_s[0] * NORM, TN) + dot3(mix_ref[1, 1], sq, TN)
+        dot3s(mix_turned[0], m_s[0] * NORM) + dot3s(mix_turned[1], sq)
     )
     h2 = hfr[4].astype(f32) + act
-    q = dot3(cm_ref[...], h2, NN)
+    q = dot3s(cm_split, h2)
     for p in range(gx_n):
-        q_send[p] = jnp.concatenate([q[cq * p : cq * p + cq]] * 2, axis=0)
-    q_recv[0] = q_send[mx]
+        q_send[p, :cq] = q[cq * p : cq * p + cq]
+    q_recv[0, :cq] = q_send[mx, :cq]
     q_copies = {}
     for d in far_row:
         dev = cell(d, 0)
@@ -569,7 +588,7 @@
         )
         q_copies[d].start()
     pending += q_copies.values()
-    r, rs = silu_pair(dot3(rh_ref[...], h2, TN))
+    r, rs = silu_pair(dot3s(rh_turned, h2))
     ro8 = jnp.broadcast_to(ro_ref[...], (8, C))
     energy = dot3(ro8, r, NN)[0:1]
     dread = dot3(rh_ref[...] * ro_ref[...], rs, NN)
@@ -641,6 +660,10 @@
             if d:
                 back(d).start()
     b_recv[mx] = b_send[0]
+    cm_turned = split2(cm_ref[...].T)
+    mix_split = [split2(mix_ref[1, p]) for p in range(2)]
+    rhi, rlo = split2(jnp.concatenate([rad_ref[1, 0], rad_ref[1, 1]], axis=1))
+    rstack = jnp.concatenate([rhi.astype(f32), rlo.astype(f32)], axis=0).astype(bf16)
     for d in range(1, gx_n):
         src = lax.rem(mx + d, gx_n)
         remote(
@@ -656,22 +679,20 @@
         long_range = long_range + b_recv[p, cq : cq + 3]
     site_ref[0] = energy + scale * colsum(q * pot)
 
-    dh = dread + dot3(cm_ref[...], pot * (2.0 * scale), TN)
+    dh = dread + dot3s(cm_turned, pot * (2.0 * scale))
     dpre = dh * slope2
-    d0 = dot3(mix_ref[1, 0], dpre, NN) * NORM
-    dsq = dot3(mix_ref[1, 1], dpre, NN) * (2.0 * NORM)
+    d0 = dot3s(mix_split[0], dpre) * NORM
+    dsq = dot3s(mix_split[1], dpre) * (2.0 * NORM)
     m_s[0] = d0
     for p in range(3):
         m_s[1 + p] = m1[p] * dsq
-    rhi, rlo = split2(jnp.concatenate([rad_ref[1, 0], rad_ref[1, 1]], axis=1))
-    rstack = jnp.concatenate([rhi.astype(f32), rlo.astype(f32)], axis=0).astype(bf16)
 
     def backward(n, _):
         u = unit_s[:, slot(n)]
         dgm, db, du = second_slot_back(
             g_s[n].astype(f32),
             w_s[n],
-            nbr_ref[n],
+            half_s[n],
             u,
             m_s[0],
             [m_s[1], m_s[2], m_s[3]],
@@ -683,25 +704,47 @@
         return 0
 
     lax.fori_loop(0, NB, backward, 0, unroll=UNROLL)
-    copies = []
-    for t in range(5):
-        part = dot(dgm_s[...], oht[t * AT : (t + 1) * AT, :], NT)
-        if t == 4:
-            grad = dh + part[:C]
-            break
-        for s, value in ((t, part[:C]), (t + 5, part[C:])):
-            g_send[s] = value.astype(bf16)
-            copies += halo(
-                2, lambda h: g_send.at[h], lambda h: g_recv.at[h], [(s // 3 - 1, s % 3 - 1)]
-            )
-    pending += copies
-    for c in copies:
+
+    def derivative(src, dst, sem_at, dev):
+        return remote(g_send.at[src], g_recv.at[dst], halo_s.at[2, sem_at], halo_r.at[2, dst], dev)
+
+    def spread_tile(t):
+        return dot(dgm_s[...], oht[t * AT : (t + 1) * AT, :], NT)
+
+    for t in (3, 4):
+        part = spread_tile(t)
+        g_send[TILES[t][0]] = part[:C].astype(bf16)
+        g_send[TILES[t][1]] = part[C:].astype(bf16)
+    shared = [derivative(inner + 1 + e, outer + 1 + e, 7 + e, cell(side, 0)) for e in (-1, 1)]
+    corners = [derivative(outer + 1 + e, inner + 1 - e, 1 + e, cell(-side, e)) for e in (-1, 1)]
+    for c in shared + corners:
+        c.start()
+    part = spread_tile(1)
+    along_x = []
+    for e, value in zip((-1, 1), (part[:C], part[C:])):
+        g_send[4 + 3 * e] = value.astype(bf16)
+        along_x.append(derivative(4 + 3 * e, 4 - 3 * e, 4 + 3 * e, cell(e, 0)))
+        along_x[-1].start()
+    part = spread_tile(2)
+    along_y = []
+    for e, value in zip((-1, 1), (part[:C], part[C:])):
+        there = inner + 1 + e
+        derivative(4, there, 7 + e, cell(side, 0)).wait_recv()
+        g_send[4 + e] = (value + g_recv[there].astype(f32)).astype(bf16)
+        along_y.append(derivative(4 + e, 4 - e, 4 + e, cell(0, e)))
+        along_y[-1].start()
+    pending += shared + corners + along_x + along_y
+    grad = dh + spread_tile(0)[:C]
+    pairs = [pair_rows(rad_ref[0, p], embed8) for p in range(2)]
+    straight = [split2(m) for m in pairs + [mix_ref[0, 0], mix_ref[0, 1]]]
+    for c in along_x + along_y:
         c.wait_recv()
-    for s in range(9):
-        if s != 4:
-            grad = grad + g_recv[s].astype(f32)
-
-    sums = layer_one_back(grad, slope1, m1_first, *layer)
+    for e in (-1, 1):
+        derivative(4, outer + 1 + e, 1 + e, cell(0, e)).wait_recv()
+        grad = grad + g_recv[outer + 1 + e].astype(f32)
+        grad = grad + g_recv[4 + e].astype(f32) + g_recv[4 + 3 * e].astype(f32)
+
+    sums = layer_one_back(grad, slope1, m1_first, *straight)
     own_grad = jnp.zeros((8, AT), f32)
     drels = []
     for n in range(NB):
@@ -712,17 +755,19 @@
         own_grad = own_grad - drel
         drels.append(drel)
     terms = [t.astype(f32) for t in split3(jnp.concatenate(drels, axis=1))]
-    far = idx >= HALF
-    terms = [jnp.where(far, 0.0, t) for t in terms] + [jnp.where(far, t, 0.0) for t in terms]
+    second = far > 0
+    terms = [jnp.where(second, 0.0, t) for t in terms] + [
+        jnp.where(second, t, 0.0) for t in terms
+    ]
     terms = jnp.concatenate(terms, axis=0).astype(bf16)
     copies = []
-    for t in range(5):
+    for t in (3, 4, 2, 1, 0):
         part = dot(terms, oht[t * AT : (t + 1) * AT, :], NT)
         low = part[:8] + part[8:16] + part[16:24]
-        if t == 4:
+        if t == 0:
             total = own_grad + low
             break
-        for s, value in ((t, low), (t + 5, part[24:32] + part[32:40] + part[40:48])):
+        for s, value in zip(TILES[t], (low, part[24:32] + part[32:40] + part[40:48])):
             f_send[s] = value
             copies += halo(
                 3,
@@ -737,9 +782,9 @@
     for s in range(9):
         if s != 4:
             total = total + f_recv[s, :3]
-    total = -(total + (2.0 * scale) * long_range)
+    total = total + (2.0 * scale) * long_range
     for p in range(3):
-        force_ref[p] = total[p : p + 1]
+        force_ref[p] = -total[p : p + 1]
 
     for c in pending:
         c.wait_send()
@@ -777,6 +822,10 @@
         vmem((gx_n, 8, AT), f32),
         vmem((9, C, AT), bf16),
         vmem((HALF, E), bf16),
+        vmem((NB, 1, AT), jnp.int32),
+        vmem((NB, 1, AT), jnp.int32),
+        vmem((NB, 2 * C, AT), f32),
+        vmem((48, E), f32),
         vmem((2 * C, HALF), bf16),
         vmem((NB, C, AT), bf16),
         vmem((NB, 2 * C, AT), f32),
@@ -813,19 +862,7 @@
         sem((gy_n,)),
         sem((KZ,)),
     ]
-    forces, site_energy = pl.pallas_call(
-        functools.partial(kernel, gx_n, gy_n),
-        out_shape=(
-            jax.ShapeDtypeStruct((3, 1, AT), f32),
-            jax.ShapeDtypeStruct((1, 1, AT), f32),
-        ),
-        in_specs=[pl.BlockSpec(memory_space=pltpu.VMEM)] * 11,
-        out_specs=(pl.BlockSpec(memory_space=pltpu.VMEM),) * 2,
-        scratch_shapes=scratch,
-        compiler_params=pltpu.CompilerParams(
-            collective_id=0, has_side_effects=True, vmem_limit_bytes=60 * 1024 * 1024
-        ),
-    )(
+    arrays = (
         jnp.transpose(positions[0], (1, 0, 2)),
         species,
         jnp.transpose(neighbours[0], (2, 0, 1)),
@@ -838,6 +875,19 @@
         charge_map.T,
         wavevectors,
     )
+    forces, site_energy = pl.pallas_call(
+        functools.partial(kernel, gx_n, gy_n),
+        out_shape=(
+            jax.ShapeDtypeStruct((3, 1, AT), f32),
+            jax.ShapeDtypeStruct((1, 1, AT), f32),
+        ),
+        in_specs=[pl.BlockSpec(memory_space=pl.ANY)] * len(arrays),
+        out_specs=(pl.BlockSpec(memory_space=pltpu.VMEM),) * 2,
+        scratch_shapes=[vmem(a.shape, a.dtype) for a in arrays] + [sem((len(arrays),))] + scratch,
+        compiler_params=pltpu.CompilerParams(
+            collective_id=0, has_side_effects=True, vmem_limit_bytes=60 * 1024 * 1024
+        ),
+    )(*arrays)
     return jnp.transpose(forces, (1, 0, 2))[None], site_energy
 
 

time: 77.3 us -> 73.7 us (0.953)
  Pallas kernels: 74.7 us -> 71.1 us
    pallas_call x1, Pallas kernels: 74.7 us -> 71.1 us  [per_device(): pl.pallas_call(functools.partial(kernel, gx_n, gy_n), out_shape=(jax.Shap...]
where the time goes in v3:
time: 73.7 us; the launch traced here: 73.6 us
  Pallas kernels  71.1 us (96%)
  local copies, waits for them, and re-layouts  1.87 us (3%)
    pallas_call x1, Pallas kernels, per_device(): pl.pallas_call(functools.partial(kernel, gx_n, gy_n), out_shape=(jax.Shap...  71.1 us
    unnamed x6, local copies, waits for them, and re-layouts  1.87 us

profile of v3, /device:TPU:1, one launch (start us, length us, event | category | flops | bytes accessed | tf_op | source)
XLA Modules:
  0.0 73.6 jit_solution(14639646421483629044)
XLA Ops:
  0.6 71.1 %shard_map.122 = (f32[3,1,256]{2,1,0:T(1,128)}, f32[1,1,256]{2,1,0:T(1,128)}) custom-call(f32[3,1,256]{2,1,0:T(1,128)} %bitcast.11, s32[1,1,256]{2,1,0:T(1,128)} %refs_1_.1, s32[12,1,256]{2,1,0:T(1,128)} %bitcast.10, s32[1,1,256]{2,1,0:T(1,128)} %refs_3_.1, f32[6,128]{1,0:T(8,128)} %refs_4_.1, f32[2,2,8,128]{3,2,1,0:T(8,128)} %refs_5_.1, ...), custom_call_target="tpu_custom_call" | custom-call | tf_op jit(solution)/shard_map/pallas_call | solution.py:878
  71.7 0.0 copy-start
  71.7 0.7 copy-done
  72.4 0.0 copy-start.1
  72.4 0.6 copy.16
  73.0 0.1 copy-done.1
  73.0 0.6 copy.17
Async XLA Ops:
  71.7 0.7 copy-start
  72.4 0.6 copy-start.1

commit v4 on v3

--- a/solution.py
+++ b/solution.py
@@ -206,20 +206,21 @@
     return jnp.concatenate([hi, lo, hi, jnp.zeros_like(hi)], axis=0).astype(bf16)
 
 
-def second_slot_back(g, w, far, unit, d0, d1, rhi, rstack):
-    w0, w1 = w[:C], w[C:]
-    ux, uy, uz = unit[0:1], unit[1:2], unit[2:3]
-    p = d1[0] * ux + d1[1] * uy + d1[2] * uz
-    dg = w0 * d0 + w1 * p
+def second_slot_source(w, far, unit, d0, d1):
+    p = d1[0] * unit[0:1] + d1[1] * unit[1:2] + d1[2] * unit[2:3]
+    dg = w[:C] * d0 + w[C:] * p
+    far = far > 0
+    return jnp.concatenate([jnp.where(far, 0.0, dg), jnp.where(far, dg, 0.0)], axis=0)
+
+
+def second_slot_back(g, w1, unit, d0, d1, rhi, rstack):
+    p = d1[0] * unit[0:1] + d1[1] * unit[1:2] + d1[2] * unit[2:3]
     xh, xl = split2(jnp.concatenate([g * d0, g * p], axis=0))
     both = dot(rstack, xh, NN)
     db = both[:8] + both[8:] + dot(rhi, xl, NN)
     t = w1 * g
     du = [colsum(t * d) for d in d1]
-    du = jnp.concatenate(du + [jnp.zeros((5, AT), f32)], axis=0)
-    far = far > 0
-    dgm = jnp.concatenate([jnp.where(far, 0.0, dg), jnp.where(far, dg, 0.0)], axis=0)
-    return dgm, db, du
+    return db, jnp.concatenate(du + [jnp.zeros((5, AT), f32)], axis=0)
 
 
 def trig8(pos_row, origin, length):
@@ -687,23 +688,14 @@
     for p in range(3):
         m_s[1 + p] = m1[p] * dsq
 
-    def backward(n, _):
-        u = unit_s[:, slot(n)]
-        dgm, db, du = second_slot_back(
-            g_s[n].astype(f32),
-            w_s[n],
-            half_s[n],
-            u,
-            m_s[0],
-            [m_s[1], m_s[2], m_s[3]],
-            rhi,
-            rstack,
+    def source_back(n, _):
+        dgm = second_slot_source(
+            w_s[n], half_s[n], unit_s[:, slot(n)], m_s[0], [m_s[1], m_s[2], m_s[3]]
         )
         dgm_s[:, slot(n)] = dgm.astype(bf16)
-        drel_s[:, slot(n)] = chain(db, du, slope_s[:, slot(n)], u, misc_s[0:1, slot(n)])
         return 0
 
-    lax.fori_loop(0, NB, backward, 0, unroll=UNROLL)
+    lax.fori_loop(0, NB, source_back, 0, unroll=UNROLL)
 
     def derivative(src, dst, sem_at, dev):
         return remote(g_send.at[src], g_recv.at[dst], halo_s.at[2, sem_at], halo_r.at[2, dst], dev)
@@ -735,6 +727,16 @@
         along_y[-1].start()
     pending += shared + corners + along_x + along_y
     grad = dh + spread_tile(0)[:C]
+
+    def edge_back(n, _):
+        u = unit_s[:, slot(n)]
+        db, du = second_slot_back(
+            g_s[n].astype(f32), w_s[n, C:], u, m_s[0], [m_s[1], m_s[2], m_s[3]], rhi, rstack
+        )
+        drel_s[:, slot(n)] = chain(db, du, slope_s[:, slot(n)], u, misc_s[0:1, slot(n)])
+        return 0
+
+    lax.fori_loop(0, NB, edge_back, 0, unroll=UNROLL)
     pairs = [pair_rows(rad_ref[0, p], embed8) for p in range(2)]
     straight = [split2(m) for m in pairs + [mix_ref[0, 0], mix_ref[0, 1]]]
     for c in along_x + along_y:

time: 73.7 us -> 72.4 us (0.982)
  Pallas kernels: 71.1 us -> 69.8 us
    pallas_call x1, Pallas kernels: 71.1 us -> 69.8 us  [per_device(): pl.pallas_call(functools.partial(kernel, gx_n, gy_n), out_shape=(jax.Shap...]
where the time goes in v4:
time: 72.4 us; the launch traced here: 72.3 us
  Pallas kernels  69.8 us (96%)
  local copies, waits for them, and re-layouts  1.87 us (3%)
    pallas_call x1, Pallas kernels, per_device(): pl.pallas_call(functools.partial(kernel, gx_n, gy_n), out_shape=(jax.Shap...  69.8 us
    unnamed x6, local copies, waits for them, and re-layouts  1.87 us

profile of v4, /device:TPU:1, one launch (start us, length us, event | category | flops | bytes accessed | tf_op | source)
XLA Modules:
  0.0 72.3 jit_solution(93766073440847453)
XLA Ops:
  0.6 69.8 %shard_map.122 = (f32[3,1,256]{2,1,0:T(1,128)}, f32[1,1,256]{2,1,0:T(1,128)}) custom-call(f32[3,1,256]{2,1,0:T(1,128)} %bitcast.11, s32[1,1,256]{2,1,0:T(1,128)} %refs_1_.1, s32[12,1,256]{2,1,0:T(1,128)} %bitcast.10, s32[1,1,256]{2,1,0:T(1,128)} %refs_3_.1, f32[6,128]{1,0:T(8,128)} %refs_4_.1, f32[2,2,8,128]{3,2,1,0:T(8,128)} %refs_5_.1, ...), custom_call_target="tpu_custom_call" | custom-call | tf_op jit(solution)/shard_map/pallas_call | solution.py:880
  70.4 0.0 copy-start
  70.4 0.7 copy-done
  71.1 0.0 copy-start.1
  71.1 0.6 copy.16
  71.7 0.1 copy-done.1
  71.7 0.6 copy.17
Async XLA Ops:
  70.4 0.7 copy-start
  71.1 0.6 copy-start.1

commit v5 on v4

--- a/solution.py
+++ b/solution.py
@@ -535,6 +535,11 @@
     cm_split, rh_turned = split2(cm_ref[...]), split2(rh_ref[...].T)
     gfold[C:, :AT] = jnp.zeros((C, AT), bf16)
     m_s[...] = jnp.zeros_like(m_s)
+    def radial_part(n, _):
+        w_s[n] = dot(left, basis_right(basis_s[:, slot(n)]), NN)
+        return 0
+
+    lax.fori_loop(0, NB, radial_part, 0, unroll=UNROLL)
     passed = []
     for c, e in zip(along_y, (-1, 1)):
         c.wait_recv()
@@ -548,7 +553,6 @@
 
     def near_part(n, _):
         part_s[n] = dot(gfold[:, :NEAR], oht[:NEAR, slot(n)], NN)
-        w_s[n] = dot(left, basis_right(basis_s[:, slot(n)]), NN)
         return 0
 
     lax.fori_loop(0, NB, near_part, 0, unroll=UNROLL)
@@ -570,7 +574,7 @@
             m_s[1 + p] += t * u[p : p + 1]
         return 0
 
-    lax.fori_loop(0, NB, forward, 0, unroll=UNROLL)
+    lax.fori_loop(0, NB, forward, 0, unroll=6)
     m1 = [m_s[1 + p] * NORM for p in range(3)]
     sq = m1[0] * m1[0] + m1[1] * m1[1] + m1[2] * m1[2]
     act, slope2 = silu_pair(

time: 72.4 us -> 72.2 us (level)
  no operation moved by 1% of the time
where the time goes in v5:
time: 72.2 us; the launch traced here: 72 us
  Pallas kernels  69.5 us (96%)
  local copies, waits for them, and re-layouts  1.87 us (3%)
    pallas_call x1, Pallas kernels, per_device(): pl.pallas_call(functools.partial(kernel, gx_n, gy_n), out_shape=(jax.Shap...  69.5 us
    unnamed x6, local copies, waits for them, and re-layouts  1.87 us

profile of v5, /device:TPU:1, one launch (start us, length us, event | category | flops | bytes accessed | tf_op | source)
XLA Modules:
  0.0 72.0 jit_solution(16535771424425747744)
XLA Ops:
  0.6 69.5 %shard_map.122 = (f32[3,1,256]{2,1,0:T(1,128)}, f32[1,1,256]{2,1,0:T(1,128)}) custom-call(f32[3,1,256]{2,1,0:T(1,128)} %bitcast.11, s32[1,1,256]{2,1,0:T(1,128)} %refs_1_.1, s32[12,1,256]{2,1,0:T(1,128)} %bitcast.10, s32[1,1,256]{2,1,0:T(1,128)} %refs_3_.1, f32[6,128]{1,0:T(8,128)} %refs_4_.1, f32[2,2,8,128]{3,2,1,0:T(8,128)} %refs_5_.1, ...), custom_call_target="tpu_custom_call" | custom-call | tf_op jit(solution)/shard_map/pallas_call | solution.py:884
  70.1 0.0 copy-start
  70.1 0.7 copy-done
  70.8 0.0 copy-start.1
  70.8 0.6 copy.16
  71.4 0.1 copy-done.1
  71.4 0.6 copy.17
Async XLA Ops:
  70.1 0.7 copy-start
  70.8 0.6 copy-start.1
